TPU v7x, 128 devices: a whole 4x4x4 slice. The times are simulated.
128 devices in a mesh: lat: 16 (over z, y_hi, core), lon: 8 (over x, y_lo).
Axes of the slice: x: 4, y: 4 (y_hi: 2, y_lo: 2; y = y_hi * 2 + y_lo), z: 4, core: 2. Of those that a mesh axis runs over, the one named last changes fastest.
Arguments:
- tokens: bfloat16 [2, 192, 384, 512], P(None, 'lat', 'lon'), may hold values from -610 to 610
- cotangent: bfloat16 [2, 192, 384, 512], P(None, 'lat', 'lon'), may hold values from -6 to 6
- w_qkv: bfloat16 [512, 1536], replicated, may hold values from -0.25 to 0.25
- w_proj: bfloat16 [512, 512], replicated, may hold values from -0.25 to 0.25
- w_up: bfloat16 [512, 2048], replicated, may hold values from -0.25 to 0.25
- w_down: bfloat16 [2048, 512], replicated, may hold values from -0.125 to 0.125
- pair_bias: float32 [8, 144, 144], replicated, may hold values from -4 to 320
- gain_one: float32 [512], replicated, may hold values from 0.5 to 1.5
- gain_two: float32 [512], replicated, may hold values from 0.5 to 1.5
Outputs:
- grad_tokens: bfloat16 [2, 192, 384, 512], P(None, 'lat', 'lon')
- grad_w_qkv: float32 [512, 1536], replicated
- grad_w_proj: float32 [512, 512], replicated
- grad_w_up: float32 [512, 2048], replicated
- grad_w_down: float32 [2048, 512], replicated
- grad_pair_bias: float32 [8, 144, 144], replicated
- grad_gain_one: float32 [512], replicated
- grad_gain_two: float32 [512], replicated
All inputs are finite; a program needn't handle non-finite values.
Results may differ from a plain program's by a relative error of at most 0.015.
Values may be sent and summed in bfloat16 or wider, within the bound.
No kernel may reach another device: no remote copies, remote signals or barrier semaphores. Data moves between devices by JAX's collectives and lax.ppermute only.
A program may use at most 128 MiB of HBM per device.

v0:
```python
import jax
import jax.numpy as jnp
from jax import lax
from jax.sharding import PartitionSpec as P

HEADS = 8
WLAT = 6
WLON = 12


EPSILON = 1e-05
MASKED = -1e30


def passed_along(array, axis, by):
    size = lax.axis_size(axis)
    return lax.ppermute(array, axis, [(i, (i + by) % size) for i in range(size)])


def layer_stats(values):
    average = jnp.mean(values, -1, keepdims=True)
    centred = values - average
    variance = jnp.mean(centred * centred, -1, keepdims=True)
    inv_std = lax.rsqrt(variance + EPSILON)
    return (centred * inv_std, inv_std)


def layer_back(grad_out, gain_vec, normed, inv_std):
    scaled = grad_out * gain_vec
    centred_grad = (
        scaled
        - jnp.mean(scaled, -1, keepdims=True)
        - normed * jnp.mean(scaled * normed, -1, keepdims=True)
    )
    return centred_grad * inv_std


def gelu_back(hidden, grad_act):
    _, pullback = jax.vjp(jax.nn.gelu, hidden)
    return pullback(grad_act)[0]


def split_windows(tensor):
    levels, height, breadth, channels = tensor.shape
    rows_win = height // WLAT
    columns_win = breadth // WLON
    tensor = tensor.reshape(levels, rows_win, WLAT, columns_win, WLON, channels)
    return tensor.transpose(1, 3, 0, 2, 4, 5).reshape(
        rows_win * columns_win, levels * WLAT * WLON, channels
    )


def join_windows(windows, levels, height, breadth):
    channels = windows.shape[-1]
    rows_win = height // WLAT
    columns_win = breadth // WLON
    windows = windows.reshape(rows_win, columns_win, levels, WLAT, WLON, channels)
    return windows.transpose(2, 0, 3, 1, 4, 5).reshape(levels, height, breadth, channels)


def to_shift(tensor):
    arrived = passed_along(tensor[:, :, : WLON // 2], "lon", -1)
    widened = jnp.concatenate([tensor[:, :, WLON // 2 :], arrived], 2)
    arrived_rows = passed_along(widened[:, : WLAT // 2], "lat", -1)
    return jnp.concatenate([widened[:, WLAT // 2 :], arrived_rows], 1)


def to_home(tensor):
    arrived = passed_along(tensor[:, -(WLAT // 2) :], "lat", 1)
    heightened = jnp.concatenate([arrived, tensor[:, : -(WLAT // 2)]], 1)
    arrived_cols = passed_along(heightened[:, :, -(WLON // 2) :], "lon", 1)
    return jnp.concatenate([arrived_cols, heightened[:, :, : -(WLON // 2)]], 2)


def window_forward(qkv_win, pair_bias, same_region):
    count_win, window_len, triple = qkv_win.shape
    features = triple // 3
    head_size = features // HEADS
    score_scale = head_size ** (-0.5)
    head_parts = qkv_win.reshape(count_win, window_len, 3, HEADS, head_size)
    scores = jnp.einsum(
        "wqhd,wkhd->whqk",
        head_parts[:, :, 0],
        head_parts[:, :, 1],
        preferred_element_type=jnp.float32,
    )
    scores = scores * score_scale + pair_bias[None]
    scores = jnp.where(same_region[:, None], scores, MASKED)
    row_top = jnp.max(scores, -1, keepdims=True)
    exponent = jnp.exp(scores - row_top)
    attention = exponent / jnp.sum(exponent, -1, keepdims=True)
    attention_low = attention.astype(jnp.bfloat16)
    mix_out = jnp.einsum(
        "whqk,wkhd->wqhd", attention_low, head_parts[:, :, 2], preferred_element_type=jnp.float32
    )
    return (
        mix_out.reshape(count_win, window_len, features).astype(jnp.bfloat16),
        attention,
        attention_low,
    )


def window_backward(qkv_win, attention, attention_low, grad_win):
    count_win, window_len, triple = qkv_win.shape
    features = triple // 3
    head_size = features // HEADS
    score_scale = head_size ** (-0.5)
    head_parts = qkv_win.reshape(count_win, window_len, 3, HEADS, head_size)
    queries = head_parts[:, :, 0]
    key_part = head_parts[:, :, 1]
    val_part = head_parts[:, :, 2]
    grad_heads = grad_win.reshape(count_win, window_len, HEADS, head_size)
    grad_probs = jnp.einsum(
        "wqhd,wkhd->whqk", grad_heads, val_part, preferred_element_type=jnp.float32
    )
    grad_val = jnp.einsum(
        "whqk,wqhd->wkhd", attention_low, grad_heads, preferred_element_type=jnp.float32
    )
    grad_scores = attention * (grad_probs - jnp.sum(grad_probs * attention, -1, keepdims=True))
    low_scores = grad_scores.astype(jnp.bfloat16)
    grad_query = (
        jnp.einsum("whqk,wkhd->wqhd", low_scores, key_part, preferred_element_type=jnp.float32)
        * score_scale
    )
    grad_key = (
        jnp.einsum("whqk,wqhd->wkhd", low_scores, queries, preferred_element_type=jnp.float32)
        * score_scale
    )
    grad_qkv = (
        jnp.stack([grad_query, grad_key, grad_val], 2)
        .reshape(count_win, window_len, triple)
        .astype(jnp.bfloat16)
    )
    return (grad_qkv, jnp.sum(grad_scores, 0))


def attn_forward(shifted, lat_rows, lat_total, gain_one, w_qkv, pair_bias):
    levels, height, breadth, features = shifted.shape
    normed, inv_std = layer_stats(shifted.astype(jnp.float32).reshape(-1, features))
    act_one = (normed * gain_one).astype(jnp.bfloat16)
    qkv = jnp.dot(act_one, w_qkv, preferred_element_type=jnp.float32).astype(jnp.bfloat16)
    qkv_win = split_windows(qkv.reshape(levels, height, breadth, 3 * features))
    region = (lat_rows >= lat_total - WLAT).astype(jnp.int32) + (
        lat_rows >= lat_total - WLAT // 2
    ).astype(jnp.int32)
    labels = split_windows(
        jnp.broadcast_to(region[None, :, None, None], (levels, height, breadth, 1))
    )[:, :, 0]
    same_region = labels[:, :, None] == labels[:, None, :]
    mix_win, attention, attention_low = window_forward(qkv_win, pair_bias, same_region)
    mix_out = join_windows(mix_win, levels, height, breadth).reshape(-1, features)
    return (mix_out, (normed, inv_std, act_one, qkv_win, attention, attention_low))


def attn_backward(saved, grad_mixed, block_dims, gain_one, w_qkv):
    normed, inv_std, act_one, qkv_win, attention, attention_low = saved
    levels, height, breadth = block_dims
    features = grad_mixed.shape[-1]
    grad_win = split_windows(grad_mixed.reshape(levels, height, breadth, features))
    grad_qkv_win, sum_bias = window_backward(qkv_win, attention, attention_low, grad_win)
    grad_qkv = join_windows(grad_qkv_win, levels, height, breadth).reshape(-1, 3 * features)
    sum_qkv = jnp.dot(act_one.T, grad_qkv, preferred_element_type=jnp.float32)
    grad_act_one = jnp.dot(grad_qkv, w_qkv.T, preferred_element_type=jnp.float32)
    sum_gain = jnp.sum(grad_act_one * normed, 0)
    grad_branch = layer_back(grad_act_one, gain_one, normed, inv_std).astype(jnp.bfloat16)
    return (grad_branch, (sum_qkv, sum_bias, sum_gain))


def mlp_part(inputs, mix_out, cotan_rows, w_proj, gain_two, w_up, w_down):
    residual = inputs.astype(jnp.float32) + jnp.dot(
        mix_out, w_proj, preferred_element_type=jnp.float32
    )
    normed, inv_std = layer_stats(residual)
    act_two = (normed * gain_two).astype(jnp.bfloat16)
    hidden = jnp.dot(act_two, w_up, preferred_element_type=jnp.float32)
    activated = jax.nn.gelu(hidden).astype(jnp.bfloat16)
    grad_act = jnp.dot(cotan_rows, w_down.T, preferred_element_type=jnp.float32)
    grad_hidden = gelu_back(hidden, grad_act).astype(jnp.bfloat16)
    sum_down = jnp.dot(activated.T, cotan_rows, preferred_element_type=jnp.float32)
    sum_up = jnp.dot(act_two.T, grad_hidden, preferred_element_type=jnp.float32)
    grad_norm = jnp.dot(grad_hidden, w_up.T, preferred_element_type=jnp.float32)
    sum_gain = jnp.sum(grad_norm * normed, 0)
    grad_residual = cotan_rows.astype(jnp.float32) + layer_back(
        grad_norm, gain_two, normed, inv_std
    )
    residual_low = grad_residual.astype(jnp.bfloat16)
    sum_proj = jnp.dot(mix_out.T, residual_low, preferred_element_type=jnp.float32)
    grad_mixed = jnp.dot(residual_low, w_proj.T, preferred_element_type=jnp.float32).astype(
        jnp.bfloat16
    )
    return (grad_residual, grad_mixed, (sum_proj, sum_up, sum_down, sum_gain))


def local(tokens, cotangent, w_qkv, w_proj, w_up, w_down, pair_bias, gain_one, gain_two):
    levels, height, breadth, features = tokens.shape
    lat_count = lax.axis_size("lat")
    lon_count = lax.axis_size("lon")
    lat_total = height * lat_count
    total_tokens = levels * height * breadth * lat_count * lon_count
    lat_rows = lax.axis_index("lat") * height + jnp.arange(height, dtype=jnp.int32)
    block_dims = (levels, height, breadth)
    block_shape = (levels, height, breadth, features)
    shifted = to_shift(tokens)
    mix_out, saved = attn_forward(shifted, lat_rows, lat_total, gain_one, w_qkv, pair_bias)
    mix_home = to_home(mix_out.reshape(block_shape)).reshape(-1, features)
    grad_residual, grad_mixed, mlp_sums = mlp_part(
        tokens.reshape(-1, features),
        mix_home,
        cotangent.reshape(-1, features),
        w_proj,
        gain_two,
        w_up,
        w_down,
    )
    grad_moved = to_shift(grad_mixed.reshape(block_shape)).reshape(-1, features)
    grad_branch, attn_sums = attn_backward(saved, grad_moved, block_dims, gain_one, w_qkv)
    returned = to_home(grad_branch.reshape(block_shape)).reshape(-1, features)
    grad_tokens = (
        (grad_residual + returned.astype(jnp.float32)).astype(jnp.bfloat16).reshape(block_shape)
    )
    sum_proj, sum_up, sum_down, sum_gain_two, sum_qkv, sum_bias, sum_gain_one = lax.psum(
        (
            mlp_sums[0],
            mlp_sums[1],
            mlp_sums[2],
            mlp_sums[3],
            attn_sums[0],
            attn_sums[1],
            attn_sums[2],
        ),
        ("lat", "lon"),
    )
    weight_scale = total_tokens ** (-0.5)
    bias_scale = levels * WLAT * WLON * weight_scale
    return (
        grad_tokens,
        sum_qkv * weight_scale,
        sum_proj * weight_scale,
        sum_up * weight_scale,
        sum_down * weight_scale,
        sum_bias * bias_scale,
        sum_gain_one * weight_scale,
        sum_gain_two * weight_scale,
    )


def solution(mesh):
    in_specs = (
        P(None, "lat", "lon", None),
        P(None, "lat", "lon", None),
        P(),
        P(),
        P(),
        P(),
        P(),
        P(),
        P(),
    )
    out_specs = (P(None, "lat", "lon", None), P(), P(), P(), P(), P(), P(), P())
    return jax.shard_map(local, mesh=mesh, in_specs=in_specs, out_specs=out_specs, check_vma=False)
```

profile of v0, /device:TPU:0, one launch (start us, length us, event | category | flops | bytes accessed | tf_op | source)
XLA Modules:
  0.0 453.4 jit_solution(11708348536479887127)
XLA Ops:
  7.2 1.1 slice.61
  8.3 3.9 collective-permute-start
  12.2 2.8 slice.60
  15.3 2.9 copy.64
  18.1 1.1 pad_maximum_fusion.5
  19.2 5.6 %collective-permute-start.1 = (bf16[2,3,48,512]{3,2,1,0:T(8,128)(2,1)S(1)}, bf16[2,3,48,512]{3,2,1,0:T(8,128)(2,1)S(1)}, u32[]{:S(2)}, u32[]{:S(2)}) collective-permute-start(bf16[2,3,48,512]{3,2,1,0:T(8,128)(2,1)S(1)} %pad_maximum_fusion.5), channel_id=1, source_target_pairs={{0,120},{8,0},{16,8},{24,16},{32,24},{40,32},{48,40},{56,48},{64,5... | collective-permute-start | bytes 884744 | tf_op jit(solution)/shard_map/ppermute | solution.py:17
  25.9 3.2 collective-permute-done.1
  30.5 0.9 copy-done.25
  31.4 3.8 convolution_convert_fusion
  35.2 6.6 %reshape_reshape.13 = bf16[2,2,6,4,12,1536]{5,4,3,2,1,0:T(8,128)(2,1)} reshape(bf16[1152,1536]{1,0:T(8,128)(2,1)} %convolution_convert_fusion) | data formatting | bytes 7077888 | tf_op jit(solution)/shard_map/reshape;reshape | solution.py:47
  41.9 6.9 %copy.60 = bf16[2,4,2,6,12,1536]{5,1,0,4,3,2:T(4,128)(2,1)} copy(bf16[2,4,2,6,12,1536]{5,4,1,3,0,2:T(8,128)(2,1)} %bitcast.101) | data formatting | bytes 7077888 | tf_op jit(solution)/shard_map/transpose | solution.py:48
  48.7 10.0 %reshape_reshape.14 = bf16[8,144,3,8,64]{4,3,2,0,1:T(8,128)(2,1)} reshape(bf16[2,4,2,6,12,1536]{5,1,0,4,3,2:T(4,128)(2,1)} %copy.60) | data formatting | bytes 7077888 | tf_op jit(solution)/shard_map/reshape;reshape | solution.py:80
  58.7 6.9 %fusion.57 = (bf16[8,144,1,8,64]{4,3,2,0,1:T(8,128)(2,1)}, bf16[8,144,1,8,64]{4,3,2,0,1:T(8,128)(2,1)}, bf16[8,144,1,8,64]{4,3,2,0,1:T(8,128)(2,1)}) fusion(bf16[8,144,3,8,64]{4,3,2,0,1:T(8,128)(2,1)} %reshape_reshape.14), kind=kLoop, calls=%fused_computation.109 | loop fusion | bytes 7077888 | tf_op jit(solution)/shard_map/slice | solution.py:83
  65.6 4.8 %copy.85 = bf16[8,144,1,8,64]{1,4,3,0,2:T(8,128)(2,1)} copy(bf16[8,144,1,8,64]{4,3,2,0,1:T(8,128)(2,1)} %get-tuple-element.31) | data formatting | bytes 2359296
  70.4 4.8 %copy.84 = bf16[8,144,1,8,64]{1,4,3,0,2:T(8,128)(2,1)} copy(bf16[8,144,1,8,64]{4,3,2,0,1:T(8,128)(2,1)} %get-tuple-element.32) | data formatting | bytes 2359296
  75.1 4.8 %copy.86 = bf16[8,144,1,8,64]{1,4,3,0,2:T(8,128)(2,1)} copy(bf16[8,144,1,8,64]{4,3,2,0,1:T(8,128)(2,1)} %get-tuple-element.33) | data formatting | bytes 2359296
  79.9 3.7 fusion.23
  83.6 6.0 %fusion.58 = (f32[8,8,144]{2,1,0:T(8,128)S(1)}, f32[8,8,144,144]{2,3,1,0:T(8,128)S(1)}) fusion(f32[8,8,144,144]{2,3,1,0:T(8,128)S(1)} %fusion.23, f32[8,144,144]{1,2,0:T(8,128)} %copy.64, pred[8,144,144]{1,2,0:T(8,128)(4,1)} %broadcast_compare_fusion), kind=kOutput, calls=%fused_computation.110 | output fusion | flops 10616975 | bytes 11483136 | tf_op jit(solution)/shard_map/sub | solution.py:90
  89.6 3.6 copy-done.7
  93.2 4.0 convert_bitcast_fusion.1
  97.2 5.1 %copy.66 = bf16[8,144,8,64]{3,2,0,1:T(8,128)(2,1)} copy(bf16[8,144,8,64]{1,3,2,0:T(8,128)(2,1)} %convert_bitcast_fusion.1) | data formatting | bytes 2359296 | tf_op jit(solution)/shard_map/convert_element_type | solution.py:97
  102.3 4.4 convert_element_type.119
  106.7 2.5 copy.67
  110.3 9.1 %collective-permute-done.2 = bf16[2,3,48,512]{3,0,2,1:T(2,128)(2,1)S(1)} collective-permute-done((bf16[2,3,48,512]{3,0,2,1:T(2,128)(2,1)S(1)}, bf16[2,3,48,512]{3,0,2,1:T(2,128)(2,1)S(1)}, u32[]{:S(2)}, u32[]{:S(2)}) %collective-permute-start.2) | collective-permute-done | bytes 294944 | tf_op jit(solution)/shard_map/ppermute | solution.py:17
  119.7 1.5 multiply_convert_fusion.4
  121.2 5.8 %collective-permute-done.3 = bf16[2,12,6,512]{3,0,2,1:T(2,128)(2,1)S(1)} collective-permute-done((bf16[2,12,6,512]{3,0,2,1:T(2,128)(2,1)S(1)}, bf16[2,12,6,512]{3,0,2,1:T(2,128)(2,1)S(1)}, u32[]{:S(2)}, u32[]{:S(2)}) %collective-permute-start.3) | collective-permute-done | bytes 147488 | tf_op jit(solution)/shard_map/ppermute | solution.py:17
  126.9 1.7 fusion.43
  130.5 2.7 fusion.56
  133.2 5.2 %fusion.12 = f32[2048,512]{1,0:T(8,128)} fusion(bf16[1152,512]{1,0:T(8,128)(2,1)S(1)} %bitcast.114, f32[1152,2048]{1,0:T(8,128)S(1)} %fusion.56), kind=kOutput, calls=%fused_computation.22 | convolution fusion | flops 2437152768 | bytes 14811136 | tf_op jit(solution)/shard_map/dot_general | solution.py:179
  138.4 8.2 %fusion.7 = bf16[1152,2048]{1,0:T(8,128)(2,1)S(1)} fusion(f32[1152,2048]{1,0:T(8,128)S(1)} %fusion.56, bf16[1152,512]{1,0:T(8,128)(2,1)S(1)} %bitcast.115, bf16[2048,512]{1,0:T(8,128)(2,1)S(1)} %copy-done.24), kind=kOutput, calls=%fused_computation.9 | convolution fusion | flops 2463105024 | bytes 17432576 | tf_op jit(solution)/shard_map/dot_general | solution.py:177
  146.7 3.4 multiply_reduce_fusion.1
  150.1 5.0 %fusion.55 = f32[512,2048]{1,0:T(8,128)} fusion(bf16[1152,2048]{1,0:T(8,128)(2,1)S(1)} %fusion.7, f32[1152,512]{1,0:T(8,128)S(1)} %get-tuple-element.37, f32[512]{0:T(512)S(1)} %copy-done.23, f32[1152]{0:T(1024)S(1)} %add_rsqrt_fusion.1, f32[1152]{0:T(1024)S(1)} %broadcast_multiply_fusion.10), kind=kOutput, calls=%fused_computation.107 | convolution fusion | flops 2418278400 | bytes 11283456 | tf_op jit(solution)/shard_map/dot_general | solution.py:180
  155.1 1.2 multiply_add_fusion
  158.0 1.1 copy_dynamic-update-slice_fusion
  159.1 4.1 collective-permute-done.4
  163.5 1.8 fusion.45
  166.0 1.7 collective-permute-done.5
  167.8 1.5 pad_maximum_fusion.4
  169.9 2.8 reshape_reshape.15
  172.7 4.8 %copy.72 = bf16[8,144,8,64]{1,3,2,0:T(8,128)(2,1)} copy(bf16[8,144,8,64]{3,2,0,1:T(8,128)(2,1)} %reshape_reshape.15) | data formatting | bytes 2359296 | tf_op jit(solution)/shard_map/reshape;reshape | solution.py:112
  177.5 7.5 %convert_bitcast_fusion = bf16[8,144,1,8,64]{1,4,3,0,2:T(8,128)(2,1)} fusion(bf16[8,144,8,64]{1,3,2,0:T(8,128)(2,1)} %copy.72, f32[8,8,144,144]{2,3,1,0:T(8,128)} %copy-done.7, f32[8,8,144]{2,1,0:T(8,128)S(1)} %get-tuple-element.34), kind=kOutput, calls=%fused_computation.61 | convolution fusion | flops 173113344 | bytes 7704576 | tf_op jit(solution)/shard_map/whqk,wqhd->wkhd/dot_general | solution.py:116
  185.0 7.0 %multiply_reduce_fusion = (f32[8,8,144]{2,1,0:T(8,128)S(1)}, f32[8,8,144,144]{2,3,1,0:T(8,128)}) fusion(f32[8,8,144,144]{2,3,1,0:T(8,128)} %copy-done.7, f32[8,8,144]{2,1,0:T(8,128)S(1)} %get-tuple-element.34, bf16[8,144,8,64]{1,3,2,0:T(8,128)(2,1)S(1)} %copy-done.11, bf16[8,144,1,8,64]{1,4,3,0,2:T(8,128)(2,1)S(1)} %copy-done.10), kind=kOutput, calls=%fused_computation.12 | convolution fusion | flops 173841408 | bytes 13049856 | tf_op jit(solution)/shard_map/wqhd,wkhd->whqk/dot_general | solution.py:113
  192.0 12.7 %fusion.14 = (f32[8,144,144]{1,2,0:T(8,128)}, bf16[8,8,144,144]{2,3,1,0:T(8,128)(2,1)}) fusion(f32[8,8,144,144]{2,3,1,0:T(8,128)} %get-tuple-element.40, f32[8,8,144]{2,1,0:T(8,128)S(1)} %get-tuple-element.39, f32[8,8,144,144]{2,3,1,0:T(8,128)} %copy-done.7, f32[8,8,144]{2,1,0:T(8,128)S(1)} %get-tuple-element.34), kind=kLoop, calls=%fused_computation.26 | loop fusion | flops 6469632 | bytes 14008320 | tf_op jit(solution)/shard_map/reduce_sum | solution.py:134
  204.6 4.8 %fusion.39 = bf16[8,144,1,8,64]{1,4,3,0,2:T(8,128)(2,1)S(1)} fusion(bf16[8,8,144,144]{2,3,1,0:T(8,128)(2,1)} %get-tuple-element.30, bf16[8,144,1,8,64]{1,4,3,0,2:T(8,128)(2,1)} %copy.85), kind=kOutput, calls=%fused_computation.66 | convolution fusion | flops 171048960 | bytes 5013504 | tf_op jit(solution)/shard_map/whqk,wqhd->wkhd/dot_general | solution.py:126
  211.2 4.1 pad_maximum_fusion
  215.3 12.0 %copy.77 = bf16[8,144,3,8,64]{4,3,2,0,1:T(8,128)(2,1)} copy(bf16[8,144,3,8,64]{1,4,3,0,2:T(8,128)(2,1)} %pad_maximum_fusion) | data formatting | bytes 7077888 | tf_op jit(solution)/shard_map/stack | solution.py:130
  227.3 10.7 %convert_element_type.125 = bf16[2,4,2,6,12,1536]{5,1,0,4,3,2:T(4,128)(2,1)} reshape(bf16[8,144,3,8,64]{4,3,2,0,1:T(8,128)(2,1)} %copy.77) | data formatting | bytes 7077888 | tf_op jit(solution)/shard_map/convert_element_type | solution.py:132
  238.0 5.4 %copy.78 = bf16[2,2,6,4,12,1536]{5,4,3,2,1,0:T(8,128)(2,1)} copy(bf16[2,2,6,4,12,1536]{5,3,1,4,2,0:T(4,128)(2,1)} %bitcast.102) | data formatting | bytes 7077888 | tf_op jit(solution)/shard_map/transpose | solution.py:58
  243.4 6.6 %reshape_reshape.16 = bf16[1152,1536]{1,0:T(8,128)(2,1)} reshape(bf16[2,2,6,4,12,1536]{5,4,3,2,1,0:T(8,128)(2,1)} %copy.78) | data formatting | bytes 7077888 | tf_op jit(solution)/shard_map/reshape;reshape | solution.py:161
  250.0 5.9 %fusion.60 = f32[512,1536]{1,0:T(8,128)} fusion(bf16[1152,512]{1,0:T(8,128)(2,1)S(1)} %bitcast.116, bf16[1152,1536]{1,0:T(8,128)(2,1)} %reshape_reshape.16), kind=kOutput, calls=%fused_computation.112 | convolution fusion | flops 1811939328 | bytes 7864320 | tf_op jit(solution)/shard_map/dot_general | solution.py:162
  256.6 5.0 %multiply_reduce_fusion.2 = (f32[512]{0:T(512)S(1)}, f32[1152]{0:T(1024)S(1)}, f32[1152]{0:T(1024)S(1)}, f32[1152,512]{1,0:T(8,128)S(1)}) fusion(f32[1152]{0:T(1024)S(1)} %copy-done.21, f32[1152]{0:T(1024)S(1)} %copy-done.19, bf16[2,3,48,512]{3,2,1,0:T(8,128)(2,1)S(1)} %collective-permute-done.1, bf16[2,9,48,512]{3,2,1,0:T(8,128)(2,1)S(1)} %fusion.44, ...), kind=kOutput, calls=%fused_computation.35 | convolution fusion | flops 1817834752 | bytes 8673280 | tf_op jit(solution)/shard_map/dot_general | solution.py:163
  261.6 1.1 multiply_convert_fusion.5
  262.8 1.0 slice.91
  263.8 67.9 %all-reduce = (f32[512]{0:T(512)S(1)}, f32[512]{0:T(512)S(1)}) all-reduce(f32[512]{0:T(512)S(1)} %get-tuple-element.18, f32[512]{0:T(512)S(1)} %get-tuple-element.16), channel_id=1, replica_groups=mesh['lat'=16,'lon'=8] {'lat','lon'}, use_global_device_ids=true, to_apply=%region_18.19 | all-reduce | flops 1024 | bytes 8192 | tf_op jit(solution)/shard_map/psum | solution.py:221
  332.3 1.0 pad_maximum_fusion.6
  333.9 8.2 %collective-permute-done.7 = bf16[2,12,6,512]{3,2,1,0:T(8,128)(2,1)S(1)} collective-permute-done((bf16[2,12,6,512]{3,2,1,0:T(8,128)(2,1)S(1)}, bf16[2,12,6,512]{3,2,1,0:T(8,128)(2,1)S(1)}, u32[]{:S(2)}, u32[]{:S(2)}) %collective-permute-start.7) | collective-permute-done | bytes 147488 | tf_op jit(solution)/shard_map/ppermute | solution.py:17
  342.1 1.7 fusion.42
  343.8 1.5 fusion.16
  345.3 85.9 %all-reduce.4.cloned.1.call-done = (f32[512,1536]{1,0:T(8,128)}, f32[512,512]{1,0:T(8,128)}, f32[512,2048]{1,0:T(8,128)}, f32[2048,512]{1,0:T(8,128)}, f32[8,144,144]{1,2,0:T(8,128)}) async-done(((f32[512,1536]{1,0:T(8,128)}, f32[512,512]{1,0:T(8,128)}, f32[512,2048]{1,0:T(8,128)}, f32[2048,512]{1,0:T(8,128)}, f32[8,144,144]{1,2,0:T(8,128)}), (f32[512,1536]{1,0:T(8,128)}, f32[512,512]{1,0:T(8,128)}, ...) | async-done | bytes 13246480 | tf_op jit(solution)/shard_map/psum | solution.py:221
  431.2 4.0 broadcast_multiply_fusion.2
  435.1 1.1 broadcast_multiply_fusion.4
  436.9 1.6 copy.79
  438.5 5.1 %broadcast_multiply_fusion.1 = f32[512,2048]{1,0:T(8,128)} fusion(f32[512,2048]{1,0:T(8,128)} %get-tuple-element.26), kind=kLoop, calls=%fused_computation.60 | loop fusion | flops 1048576 | bytes 8388608 | tf_op jit(solution)/shard_map/mul | solution.py:239
  443.6 2.5 broadcast_multiply_fusion
  (96 shorter events, 13.6 us)
Async XLA Ops:
  7.2 123.1 %copy-start = (bf16[512,2048]{1,0:T(8,128)(2,1)S(1)}, bf16[512,2048]{1,0:T(8,128)(2,1)}, u32[]{:S(2)}) copy-start(bf16[512,2048]{1,0:T(8,128)(2,1)} %param.13) | copy-start | bytes 6291460
  7.2 424.0 %all-reduce.4.cloned.1.call-start = ((), (), s32[]{:S(2)}) async-start(), calls=%async_computation | async-start | bytes 27525120 | tf_op jit(solution)/shard_map/psum | solution.py:221
  8.3 9.8 %collective-permute-start = (bf16[2,12,6,512]{3,2,1,0:T(8,128)(2,1)S(1)}, bf16[2,12,6,512]{3,2,1,0:T(8,128)(2,1)S(1)}, u32[]{:S(2)}, u32[]{:S(2)}) collective-permute-start(bf16[2,12,6,512]{3,2,1,0:T(8,128)(2,1)S(1)} %slice.61), channel_id=1, source_target_pairs={{0,7},{1,0},{2,1},{3,2},{4,3},{5,4},{6,5},{7,6},{8,15},{9,8},{10,9... | collective-permute-start | bytes 442376 | tf_op jit(solution)/shard_map/ppermute | solution.py:17
  18.1 7.6 %copy-start.6 = (bf16[2,12,42,512]{3,2,1,0:T(8,128)(2,1)S(1)}, bf16[2,12,42,512]{3,2,1,0:T(8,128)(2,1)}, u32[]{:S(2)}) copy-start(bf16[2,12,42,512]{3,2,1,0:T(8,128)(2,1)} %slice.60) | copy-start | bytes 3096580
  19.2 9.8 %collective-permute-start.1 = (bf16[2,3,48,512]{3,2,1,0:T(8,128)(2,1)S(1)}, bf16[2,3,48,512]{3,2,1,0:T(8,128)(2,1)S(1)}, u32[]{:S(2)}, u32[]{:S(2)}) collective-permute-start(bf16[2,3,48,512]{3,2,1,0:T(8,128)(2,1)S(1)} %pad_maximum_fusion.5), channel_id=1, source_target_pairs={{0,120},{8,0},{16,8},{24,16},{32,24},{40,32},{48,40},{56,48},{64,5... | collective-permute-start | bytes 884744 | tf_op jit(solution)/shard_map/ppermute | solution.py:17
  25.8 4.3 copy-start.22
  29.4 5.9 %copy-start.18 = (f32[1152]{0:T(1024)}, f32[1152]{0:T(1024)S(1)}, u32[]{:S(2)}) copy-start(f32[1152]{0:T(1024)S(1)} %div.35) | copy-start | bytes 13828
  30.0 5.2 %copy-start.20 = (f32[1152]{0:T(1024)}, f32[1152]{0:T(1024)S(1)}, u32[]{:S(2)}) copy-start(f32[1152]{0:T(1024)S(1)} %rsqrt.21) | copy-start | bytes 13828
  30.0 1.4 copy-start.25
  89.5 3.6 copy-start.7
  109.4 10.0 %collective-permute-start.2 = (bf16[2,3,48,512]{3,0,2,1:T(2,128)(2,1)S(1)}, bf16[2,3,48,512]{3,0,2,1:T(2,128)(2,1)S(1)}, u32[]{:S(2)}, u32[]{:S(2)}) collective-permute-start(bf16[2,3,48,512]{3,0,2,1:T(2,128)(2,1)S(1)} %slice.84), channel_id=1, source_target_pairs={{0,8},{8,16},{16,24},{24,32},{32,40},{40,48},{48,56},{56,64},{64,7... | collective-permute-start | bytes 884744 | tf_op jit(solution)/shard_map/ppermute | solution.py:17
  119.6 7.3 %collective-permute-start.3 = (bf16[2,12,6,512]{3,0,2,1:T(2,128)(2,1)S(1)}, bf16[2,12,6,512]{3,0,2,1:T(2,128)(2,1)S(1)}, u32[]{:S(2)}, u32[]{:S(2)}) collective-permute-start(bf16[2,12,6,512]{3,0,2,1:T(2,128)(2,1)S(1)} %pad_maximum_fusion.7), channel_id=1, source_target_pairs={{0,1},{1,2},{2,3},{3,4},{4,5},{5,6},{6,7},{7,0},{8,9},{9,10},{10,1... | collective-permute-start | bytes 442376 | tf_op jit(solution)/shard_map/ppermute | solution.py:17
  121.2 7.7 %copy-start.8 = (bf16[2,12,48,512]{3,2,1,0:T(8,128)(2,1)S(1)}, bf16[2,12,48,512]{3,2,1,0:T(8,128)(2,1)}, u32[]{:S(2)}) copy-start(bf16[2,12,48,512]{3,2,1,0:T(8,128)(2,1)} %param.9) | copy-start | bytes 3538948
  121.2 7.7 %copy-start.13 = (bf16[512,512]{1,0:T(8,128)(2,1)S(1)}, bf16[512,512]{1,0:T(8,128)(2,1)}, u32[]{:S(2)}) copy-start(bf16[512,512]{1,0:T(8,128)(2,1)} %param.12) | copy-start | bytes 1572868
  129.8 0.7 copy-start.23
  130.5 2.7 copy-start.14
  133.2 5.3 %copy-start.24 = (bf16[2048,512]{1,0:T(8,128)(2,1)S(1)}, bf16[2048,512]{1,0:T(8,128)(2,1)}, u32[]{:S(2)}) copy-start(bf16[2048,512]{1,0:T(8,128)(2,1)} %param.14) | copy-start | bytes 6291460
  156.3 7.2 %copy-start.4 = (f32[1152,512]{1,0:T(8,128)}, f32[1152,512]{1,0:T(8,128)S(1)}, u32[]{:S(2)}) copy-start(f32[1152,512]{1,0:T(8,128)S(1)} %multiply_add_fusion) | copy-start | bytes 7077892
  157.9 5.2 %collective-permute-start.4 = (bf16[2,12,6,512]{3,0,2,1:T(2,128)(2,1)S(1)}, bf16[2,12,6,512]{3,0,2,1:T(2,128)(2,1)S(1)}, u32[]{:S(2)}, u32[]{:S(2)}) collective-permute-start(bf16[2,12,6,512]{3,0,2,1:T(2,128)(2,1)S(1)} %copy.88), channel_id=1, source_target_pairs={{0,7},{1,0},{2,1},{3,2},{4,3},{5,4},{6,5},{7,6},{8,15},{9,8},{10,9... | collective-permute-start | bytes 442376 | tf_op jit(solution)/shard_map/ppermute | solution.py:17
  163.4 4.3 collective-permute-start.5
  177.5 7.5 %copy-start.10 = (bf16[8,144,1,8,64]{1,4,3,0,2:T(8,128)(2,1)S(1)}, bf16[8,144,1,8,64]{1,4,3,0,2:T(8,128)(2,1)}, u32[]{:S(2)}) copy-start(bf16[8,144,1,8,64]{1,4,3,0,2:T(8,128)(2,1)} %copy.84) | copy-start | bytes 3538948
  177.5 7.5 %copy-start.11 = (bf16[8,144,8,64]{1,3,2,0:T(8,128)(2,1)S(1)}, bf16[8,144,8,64]{1,3,2,0:T(8,128)(2,1)}, u32[]{:S(2)}) copy-start(bf16[8,144,8,64]{1,3,2,0:T(8,128)(2,1)} %copy.72) | copy-start | bytes 3538948
  204.6 4.8 %copy-start.2 = (bf16[8,8,144,144]{2,3,1,0:T(8,128)(2,1)S(1)}, bf16[8,8,144,144]{2,3,1,0:T(8,128)(2,1)}, u32[]{:S(2)}) copy-start(bf16[8,8,144,144]{2,3,1,0:T(8,128)(2,1)} %get-tuple-element.30) | copy-start | bytes 7962628
  204.6 5.0 %copy-start.3 = (bf16[8,144,1,8,64]{1,4,3,0,2:T(8,128)(2,1)S(1)}, bf16[8,144,1,8,64]{1,4,3,0,2:T(8,128)(2,1)}, u32[]{:S(2)}) copy-start(bf16[8,144,1,8,64]{1,4,3,0,2:T(8,128)(2,1)} %copy.86) | copy-start | bytes 3538948
  209.6 1.6 copy-start.12
  243.4 6.6 %copy-start.16 = (bf16[2,12,48,512]{3,2,1,0:T(8,128)(2,1)S(1)}, bf16[2,12,48,512]{3,2,1,0:T(8,128)(2,1)}, u32[]{:S(2)}) copy-start(bf16[2,12,48,512]{3,2,1,0:T(8,128)(2,1)} %multiply_convert_fusion.4) | copy-start | bytes 3538948
  255.9 0.7 copy-start.19
  255.9 0.7 copy-start.21
  262.7 69.5 %collective-permute-start.6 = (bf16[2,3,48,512]{3,2,1,0:T(8,128)(2,1)S(1)}, bf16[2,3,48,512]{3,2,1,0:T(8,128)(2,1)S(1)}, u32[]{:S(2)}, u32[]{:S(2)}) collective-permute-start(bf16[2,3,48,512]{3,2,1,0:T(8,128)(2,1)S(1)} %slice.90), channel_id=1, source_target_pairs={{0,8},{8,16},{16,24},{24,32},{32,40},{40,48},{48,56},{56,64},{64,7... | collective-permute-start | bytes 884744 | tf_op jit(solution)/shard_map/ppermute | solution.py:17
  263.8 80.0 %copy-start.5 = (f32[1152,512]{1,0:T(8,128)S(1)}, f32[1152,512]{1,0:T(8,128)}, u32[]{:S(2)}) copy-start(f32[1152,512]{1,0:T(8,128)} %copy-done.4) | copy-start | bytes 7077892
  333.2 8.9 %collective-permute-start.7 = (bf16[2,12,6,512]{3,2,1,0:T(8,128)(2,1)S(1)}, bf16[2,12,6,512]{3,2,1,0:T(8,128)(2,1)S(1)}, u32[]{:S(2)}, u32[]{:S(2)}) collective-permute-start(bf16[2,12,6,512]{3,2,1,0:T(8,128)(2,1)S(1)} %pad_maximum_fusion.6), channel_id=1, source_target_pairs={{0,1},{1,2},{2,3},{3,4},{4,5},{5,6},{6,7},{7,0},{8,9},{9,10},{10,1... | collective-permute-start | bytes 442376 | tf_op jit(solution)/shard_map/ppermute | solution.py:17
  431.2 4.0 copy-start.17
  435.1 1.6 copy-start.15
  438.5 5.1 %copy-start.9 = (f32[2048,512]{1,0:T(8,128)S(1)}, f32[2048,512]{1,0:T(8,128)}, u32[]{:S(2)}) copy-start(f32[2048,512]{1,0:T(8,128)} %get-tuple-element.27) | copy-start | bytes 12582916
  443.6 2.5 copy-start.1
Sparse Core Ops, SparseCore 0:
  256.0 175.1 all-reduce.3
where the time goes:
time: 460 us; the launch traced here: 453 us
  local copies, waits for them, and re-layouts  120 us (26%)
  waiting for transfers between devices  118 us (26%)
  matrix products  70.5 us (15%)
  blocking collectives  67.9 us (15%)
  other arithmetic  51.8 us (11%)
  between operations  14.9 us (3%)
  starting transfers between devices  10 us (2%)
    psum x1, waiting for transfers between devices, local(): lax.psum((mlp_sums[0], mlp_sums[1], mlp_sums[2], mlp_sums[3], attn_sums[0...  85.9 us
    psum x1, blocking collectives, local(): lax.psum((mlp_sums[0], mlp_sums[1], mlp_sums[2], mlp_sums[3], attn_sums[0...  67.9 us
    ppermute x8, waiting for transfers between devices, passed_along(): lax.ppermute(array, axis, [(i, (i + by) % size) for i in range(size)])  32.1 us
    unnamed x59, local copies, waits for them, and re-layouts  27.1 us
    reduce_sum x1, other arithmetic, window_backward(): return (grad_qkv, jnp.sum(grad_scores, 0))  12.7 us
    another operation x1, local copies, waits for them, and re-layouts, window_backward(): jnp.stack([grad_query, grad_key, grad_val], 2)  12 us
    convert_element_type x1, local copies, waits for them, and re-layouts, window_backward(): grad_qkv = jnp.stack([grad_query, grad_key, grad_val], 2).reshape(count_w...  10.7 us
    ppermute x8, starting transfers between devices, passed_along(): lax.ppermute(array, axis, [(i, (i + by) % size) for i in range(size)])  9.97 us
  transfers between devices with their start and end apart: 9, of which 7 were waited for; matrix products, arithmetic and copies ran while one was open for 6% of the time, Pallas kernels for 0%

commit v1 on v0

v1 whole, which is shorter than its diff:
```python
import functools

import jax
import jax.numpy as jnp
from jax import lax
from jax.experimental import pallas as pl
from jax.experimental.pallas import tpu as pltpu
from jax.sharding import PartitionSpec as P

HEADS = 8
WLAT = 6
WLON = 12
WT = 144
D = 512
QKV = 1536
FF = 2048
LEVELS = 2
HEIGHT = 12
BREADTH = 48
WINDOWS = 8
ROWS = WINDOWS * WT
EPSILON = 1e-05
MASKED = -1e30
F32 = jnp.float32
BF16 = jnp.bfloat16
PIECES = 32
ONE_ROWS = 512
TWO_ROWS = 304
PROJ_AT = 6144
BIAS_AT = 8192
REST_AT = 9344
GAIN_AT = 9488
TWO_TOTAL = PIECES * TWO_ROWS
VMEM_LIMIT = 56 * 1024 * 1024

NN = (((1,), (0,)), ((), ()))
NT = (((1,), (1,)), ((), ()))
TN = (((0,), (0,)), ((), ()))


def mm(a, b, dims=NN):
    return lax.dot_general(a, b, dims, preferred_element_type=F32)


def stats_of(values):
    average = jnp.mean(values, -1, keepdims=True)
    centred = values - average
    variance = jnp.mean(centred * centred, -1, keepdims=True)
    inv_std = lax.rsqrt(variance + EPSILON)
    return centred * inv_std, inv_std


def back_of(grad_out, gain_vec, normed, inv_std):
    scaled = grad_out * gain_vec
    return (
        scaled
        - jnp.mean(scaled, -1, keepdims=True)
        - normed * jnp.mean(scaled * normed, -1, keepdims=True)
    ) * inv_std


def run_at(level, row, column):
    window = (row // WLAT) * 4 + column
    return window * WT + level * (WT // 2) + (row % WLAT) * WLON


def gather_windows(main_ref, lon_ref, lat_ref, both_ref, line, wide, out_ref):
    for level in range(LEVELS):
        for row in range(HEIGHT):
            if row < HEIGHT - WLAT // 2:
                line[0:BREADTH] = main_ref[level, row + WLAT // 2].astype(F32)
                line[BREADTH : BREADTH + 6] = lon_ref[level, row + WLAT // 2].astype(F32)
            else:
                line[0:BREADTH] = lat_ref[level, row - (HEIGHT - WLAT // 2)].astype(F32)
                line[BREADTH : BREADTH + 6] = both_ref[level, row - (HEIGHT - WLAT // 2)].astype(F32)
            for column in range(4):
                at = run_at(level, row, column)
                wide[at : at + WLON] = line[6 + WLON * column : 18 + WLON * column]

    def narrow(window, _):
        rows = pl.ds(pl.multiple_of(window * WT, 16), WT)
        out_ref[rows] = wide[rows].astype(BF16)
        return 0

    lax.fori_loop(0, WINDOWS, narrow, 0)


def slot_of(place_ref, block):
    core = block // 16
    return (
        ((core + 2 - place_ref[0]) % 2) * 16
        + (((block // 4) % 4 + 4 - place_ref[1 + core]) % 4) * 4
        + (block % 4 + 4 - place_ref[2 + core]) % 4
    )


def slot_from(place_ref, block):
    core = block // 16
    return (
        ((place_ref[0] + 2 - core) % 2) * 16
        + ((place_ref[1 + core] + 4 - (block // 4) % 4) % 4) * 4
        + (place_ref[2 + core] + 4 - block % 4) % 4
    )


def window_rows(window):
    return pl.ds(pl.multiple_of(window * WT, 16), WT)


def forward_kernel(
    place_ref, tok, tok_lon, tok_lat, tok_both, cot, cot_lon, cot_lat, cot_both,
    w_qkv, w_proj, w_up, w_down, bias_t, mask_t, gain_one, gain_two,
    xw, qkv, probs, grad_mixed, grad_res, sums_one, sum_proj, sum_gain,
    line, wide, cotw, act, mix, normed, inv_two, act_t, activated, grad_hidden, grad_norm,
):
    gather_windows(tok, tok_lon, tok_lat, tok_both, line, wide, xw)
    gather_windows(cot, cot_lon, cot_lat, cot_both, line, wide, cotw)

    def norm_one(window, _):
        rows = window_rows(window)
        values, _ = stats_of(xw[rows].astype(F32))
        act[rows] = (values * gain_one[...]).astype(BF16)
        return 0

    lax.fori_loop(0, WINDOWS, norm_one, 0)

    def project(n, _):
        cols = pl.ds(pl.multiple_of(n * 256, 256), 256)
        qkv[:, cols] = mm(act[...], w_qkv[:, cols]).astype(BF16)
        return 0

    lax.fori_loop(0, QKV // 256, project, 0)

    lane = lax.broadcasted_iota(jnp.int32, (1, 128), 1)
    first = lane < 64
    halves = (first.astype(BF16), (lane >= 64).astype(BF16))

    def attend(window, _):
        rows = window_rows(window)
        for pair in range(HEADS // 2):
            cols = slice(128 * pair, 128 * pair + 128)
            query = qkv[rows, cols]
            key = qkv[rows, 512 + 128 * pair : 640 + 128 * pair]
            val = qkv[rows, 1024 + 128 * pair : 1152 + 128 * pair]
            mixed = []
            for half in range(2):
                head = 2 * pair + half
                scores = mm(key, query * halves[half], NT) * 0.125 + bias_t[head]
                scores = scores + jnp.where(window >= 4, mask_t[...], 0.0)
                top = jnp.max(scores, 0, keepdims=True)
                exponent = jnp.exp(scores - top)
                total = jnp.sum(exponent, 0, keepdims=True)
                weights = (exponent * (1.0 / total)).astype(BF16)
                probs[window, head] = weights
                mixed.append(mm(weights, val, TN))
            mix[rows, cols] = jnp.where(first, mixed[0], mixed[1]).astype(BF16)
        return 0

    lax.fori_loop(0, WINDOWS, attend, 0)

    def norm_two(window, _):
        rows = window_rows(window)
        residual = xw[rows].astype(F32) + mm(mix[rows], w_proj[...])
        values, inv_std = stats_of(residual)
        normed[rows] = values
        inv_two[rows] = inv_std
        act[rows] = (values * gain_two[...]).astype(BF16)
        grad_norm[rows] = jnp.zeros((WT, D), F32)
        return 0

    lax.fori_loop(0, WINDOWS, norm_two, 0)
    act_t[...] = act[...].T

    c0 = 0.7978845608028654
    c1 = c0 * 0.044715

    def mlp(f, _):
        cols = pl.ds(pl.multiple_of(f * 512, 512), 512)

        def rows_of(r, _):
            rows = pl.ds(pl.multiple_of(r * WT, 16), WT)
            u = mm(act[rows], w_up[:, cols])
            grad_act = mm(cotw[rows], w_down[cols, :], NT)
            square = u * u
            gate = 0.5 + 0.5 * jnp.tanh(u * (c0 + c1 * square))
            value = u * gate
            activated[rows] = value.astype(BF16)
            slope = gate + value * (1.0 - gate) * (2.0 * c0 + 6.0 * c1 * square)
            grad_hidden[rows] = (grad_act * slope).astype(BF16)
            return 0

        lax.fori_loop(0, WINDOWS, rows_of, 0)
        down = mm(activated[...], cotw[...], TN).astype(BF16)
        for j in range(4):
            sums_one[slot_of(place_ref, 16 + f * 4 + j)] = down[:, 128 * j : 128 * j + 128]
        up = mm(act_t[...], grad_hidden[...]).astype(BF16)
        for j in range(4):
            sums_one[slot_of(place_ref, f * 4 + j)] = up[:, 128 * j : 128 * j + 128]

        def norm_rows(r, _):
            rows = pl.ds(pl.multiple_of(r * WT, 16), WT)
            grad_norm[rows] += mm(grad_hidden[rows], w_up[:, cols], NT)
            return 0

        lax.fori_loop(0, WINDOWS, norm_rows, 0)
        return 0

    lax.fori_loop(0, FF // 512, mlp, 0)

    def back(window, total):
        rows = window_rows(window)
        grads = grad_norm[rows]
        values = normed[rows]
        total = total + jnp.sum(grads * values, 0, keepdims=True)
        residual = cotw[rows].astype(F32) + back_of(grads, gain_two[...], values, inv_two[rows])
        grad_res[rows] = residual
        low = residual.astype(BF16)
        act[rows] = low
        grad_mixed[rows] = mm(low, w_proj[...], NT).astype(BF16)
        return total

    sum_gain[...] = lax.fori_loop(0, WINDOWS, back, jnp.zeros((1, D), F32))
    proj = mm(mix[...], act[...], TN).astype(BF16)
    for j in range(4):
        sum_proj[j] = proj[:, 128 * j : 128 * j + 128]


def backward_kernel(
    place_ref, xw, qkv, probs, grad_mixed, grad_res, sum_proj, sum_gain_two, w_qkv, gain_one,
    grad_grid, sums_two,
    act, act_t, grad_qkv, bias_acc, wide, line, flat,
):
    lane = lax.broadcasted_iota(jnp.int32, (1, 128), 1)
    first = lane < 64
    halves = (first.astype(BF16), (lane >= 64).astype(BF16))
    bias_acc[...] = jnp.zeros_like(bias_acc)

    def attend(window, _):
        rows = window_rows(window)
        for pair in range(HEADS // 2):
            cols = slice(128 * pair, 128 * pair + 128)
            kcols = slice(512 + 128 * pair, 640 + 128 * pair)
            vcols = slice(1024 + 128 * pair, 1152 + 128 * pair)
            query = qkv[rows, cols]
            key = qkv[rows, kcols]
            val = qkv[rows, vcols]
            out = grad_mixed[rows, cols]
            got = []
            for half in range(2):
                head = 2 * pair + half
                grad_probs = mm(val, out * halves[half], NT)
                low_probs = probs[window, head]
                weights = low_probs.astype(F32)
                product = grad_probs * weights
                grads = product - weights * jnp.sum(product, 0, keepdims=True)
                bias_acc[head] += grads
                low = grads.astype(BF16)
                got.append((mm(low, key, TN), mm(low, query), mm(low_probs, out)))
            grad_qkv[rows, cols] = (jnp.where(first, got[0][0], got[1][0]) * 0.125).astype(BF16)
            grad_qkv[rows, kcols] = (jnp.where(first, got[0][1], got[1][1]) * 0.125).astype(BF16)
            grad_qkv[rows, vcols] = jnp.where(first, got[0][2], got[1][2]).astype(BF16)
        return 0

    lax.fori_loop(0, WINDOWS, attend, 0)

    def branch(window, total):
        rows = window_rows(window)
        values, inv_std = stats_of(xw[rows].astype(F32))
        act[rows] = (values * gain_one[...]).astype(BF16)
        grads = mm(grad_qkv[rows], w_qkv[...], NT)
        total = total + jnp.sum(grads * values, 0, keepdims=True)
        low = back_of(grads, gain_one[...], values, inv_std).astype(BF16)
        wide[rows] = grad_res[rows] + low.astype(F32)
        return total

    total = lax.fori_loop(0, WINDOWS, branch, jnp.zeros((1, D), F32))
    act_t[...] = act[...].T

    def weights(n, _):
        cols = pl.ds(pl.multiple_of(n * 256, 256), 256)
        part = mm(act_t[...], grad_qkv[:, cols]).astype(BF16)
        for j in range(2):
            at = pl.multiple_of((n * 2 + j) * 512, 512)
            flat[pl.ds(at, 512)] = part[:, 128 * j : 128 * j + 128]
        return 0

    lax.fori_loop(0, QKV // 256, weights, 0)
    for j in range(4):
        flat[PROJ_AT + 512 * j : PROJ_AT + 512 * j + 512] = sum_proj[j]
    for head in range(HEADS):
        at = BIAS_AT + WT * head
        flat[at : at + WT] = bias_acc[head, :, 0:128].astype(BF16)
    rest = jnp.concatenate([bias_acc[head, :, 128:144] for head in range(HEADS)], 1)
    flat[REST_AT : REST_AT + WT] = rest.astype(BF16)
    gains = [v[:, 128 * j : 128 * j + 128] for v in (total, sum_gain_two[...]) for j in range(4)]
    gains = jnp.concatenate(gains + [jnp.zeros((8, 128), F32)], 0)
    flat[GAIN_AT : GAIN_AT + 16] = gains.astype(BF16)
    flat[GAIN_AT + 16 :] = jnp.zeros((TWO_TOTAL - GAIN_AT - 16, 128), BF16)
    for piece in range(PIECES):
        sums_two[slot_of(place_ref, piece)] = flat[piece * TWO_ROWS : (piece + 1) * TWO_ROWS]

    for level in range(LEVELS):
        for row in range(HEIGHT):
            for column in range(4):
                at = run_at(level, row, column)
                line[WLON * column : WLON * column + WLON] = wide[at : at + WLON]
            grad_grid[level, row] = line[0:BREADTH].astype(BF16)


def finish_one_kernel(scale, place_ref, up_in, down_in, up_out, down_out):
    up_out[...] = up_in[0].astype(F32) * scale
    down_out[...] = down_in[0].astype(F32) * scale


def finish_two_kernel(scale, place_ref, sums, qkv, proj, bias, gain_one, gain_two, flat, arrived):
    copies = []
    for piece in range(PIECES):
        copy = pltpu.make_async_copy(
            sums.at[slot_from(place_ref, piece), pl.ds(ONE_ROWS, TWO_ROWS)],
            flat.at[pl.ds(piece * TWO_ROWS, TWO_ROWS)],
            arrived.at[piece],
        )
        copy.start()
        copies.append(copy)
    for copy in copies:
        copy.wait()
    for j in range(12):
        qkv[:, 128 * j : 128 * j + 128] = flat[512 * j : 512 * j + 512].astype(F32) * scale
    for j in range(4):
        at = PROJ_AT + 512 * j
        proj[:, 128 * j : 128 * j + 128] = flat[at : at + 512].astype(F32) * scale
    rest = flat[REST_AT : REST_AT + WT].astype(F32) * (scale * WT)
    for head in range(HEADS):
        at = BIAS_AT + WT * head
        bias[head, :, 0:128] = flat[at : at + WT].astype(F32) * (scale * WT)
        bias[head, :, 128:144] = rest[:, 16 * head : 16 * head + 16]
    gains = flat[GAIN_AT : GAIN_AT + 16].astype(F32) * scale
    for j in range(4):
        gain_one[:, 128 * j : 128 * j + 128] = gains[j : j + 1]
        gain_two[:, 128 * j : 128 * j + 128] = gains[4 + j : 5 + j]


def shape(*dims, dtype=BF16):
    return jax.ShapeDtypeStruct(dims, dtype)


def params():
    return pltpu.CompilerParams(vmem_limit_bytes=VMEM_LIMIT)


def specs(count):
    return [pl.BlockSpec(memory_space=pltpu.SMEM)] + [
        pl.BlockSpec(memory_space=pltpu.VMEM) for _ in range(count)
    ]


def forward(*operands):
    return pl.pallas_call(
        forward_kernel,
        out_shape=(
            shape(ROWS, D), shape(ROWS, QKV), shape(WINDOWS, HEADS, WT, WT), shape(ROWS, D),
            shape(ROWS, D, dtype=F32), shape(PIECES, ONE_ROWS, 128), shape(4, 512, 128),
            shape(1, D, dtype=F32),
        ),
        in_specs=specs(len(operands) - 1),
        scratch_shapes=[
            pltpu.VMEM((56, D), F32),
            pltpu.VMEM((ROWS, D), F32),
            pltpu.VMEM((ROWS, D), BF16),
            pltpu.VMEM((ROWS, D), BF16),
            pltpu.VMEM((ROWS, D), BF16),
            pltpu.VMEM((ROWS, D), F32),
            pltpu.VMEM((ROWS, 1), F32),
            pltpu.VMEM((D, ROWS), BF16),
            pltpu.VMEM((ROWS, 512), BF16),
            pltpu.VMEM((ROWS, 512), BF16),
            pltpu.VMEM((ROWS, D), F32),
        ],
        compiler_params=params(),
        name="forward_mlp",
    )(*operands)


def backward(*operands):
    return pl.pallas_call(
        backward_kernel,
        out_shape=(shape(LEVELS, HEIGHT, BREADTH, D), shape(PIECES, TWO_ROWS, 128)),
        in_specs=specs(len(operands) - 1),
        scratch_shapes=[
            pltpu.VMEM((ROWS, D), BF16),
            pltpu.VMEM((D, ROWS), BF16),
            pltpu.VMEM((ROWS, QKV), BF16),
            pltpu.VMEM((HEADS, WT, WT), F32),
            pltpu.VMEM((ROWS, D), F32),
            pltpu.VMEM((48, D), F32),
            pltpu.VMEM((TWO_TOTAL, 128), BF16),
        ],
        compiler_params=params(),
        name="attention_back",
    )(*operands)


def finish_one(place, sums, scale):
    return pl.pallas_call(
        functools.partial(finish_one_kernel, scale),
        out_shape=(shape(D, FF, dtype=F32), shape(FF, D, dtype=F32)),
        grid_spec=pltpu.PrefetchScalarGridSpec(
            num_scalar_prefetch=1,
            grid=(16,),
            in_specs=[
                pl.BlockSpec((1, 512, 128), lambda i, place: (slot_from(place, i), 0, 0)),
                pl.BlockSpec((1, 512, 128), lambda i, place: (slot_from(place, i + 16), 0, 0)),
            ],
            out_specs=[
                pl.BlockSpec((512, 128), lambda i, place: (0, i)),
                pl.BlockSpec((512, 128), lambda i, place: (i // 4, i % 4)),
            ],
        ),
        compiler_params=params(),
        name="finish_mlp",
    )(place, sums, sums)


def finish_two(place, sums, scale):
    return pl.pallas_call(
        functools.partial(finish_two_kernel, scale),
        out_shape=(
            shape(D, QKV, dtype=F32), shape(D, D, dtype=F32), shape(HEADS, WT, WT, dtype=F32),
            shape(1, D, dtype=F32), shape(1, D, dtype=F32),
        ),
        in_specs=[pl.BlockSpec(memory_space=pltpu.SMEM), pl.BlockSpec(memory_space=pl.ANY)],
        scratch_shapes=[
            pltpu.VMEM((TWO_TOTAL, 128), BF16),
            pltpu.SemaphoreType.DMA((PIECES,)),
        ],
        compiler_params=params(),
        name="finish_attention",
    )(place, sums)


def neighbour(array, lat_by, lon_by):
    lat_count, lon_count = lax.axis_size("lat"), lax.axis_size("lon")
    pairs = []
    for i in range(lat_count):
        for j in range(lon_count):
            to = ((i + lat_by) % lat_count) * lon_count + (j + lon_by) % lon_count
            pairs.append((i * lon_count + j, to))
    return lax.ppermute(array, ("lat", "lon"), pairs)


def halos(tensor):
    edge, top = WLON // 2, WLAT // 2
    return (
        neighbour(tensor[:, :, :edge], 0, -1),
        neighbour(tensor[:, :top], -1, 0),
        neighbour(tensor[:, :top, :edge], -1, -1),
    )


def bring_home(grid):
    edge, top = WLON // 2, WLAT // 2
    from_lon = neighbour(grid[:, :-top, -edge:], 0, 1)
    from_lat = neighbour(grid[:, -top:, :-edge], 1, 0)
    from_both = neighbour(grid[:, -top:, -edge:], 1, 1)
    upper = jnp.concatenate([from_both, from_lat], 2)
    lower = jnp.concatenate([from_lon, grid[:, :-top, :-edge]], 2)
    return jnp.concatenate([upper, lower], 1)


def position(lat, lon):
    return lat % 2, (lon // 2, (lat // 2) % 2 * 2 + lon % 2, lat // 4)


ORDERS = ((0, 1, 2), (1, 2, 0))


def place_of():
    core, chip = position(lax.axis_index("lat"), lax.axis_index("lon"))
    return jnp.stack([core, *chip]).astype(jnp.int32)


def along(array, stage, by):
    pairs = []
    for lat in range(16):
        for lon in range(8):
            core, chip = position(lat, lon)
            chip = list(chip)
            axis = ORDERS[core][stage]
            chip[axis] = (chip[axis] + by) % 4
            x, y, z = chip
            to = (z * 4 + y // 2 * 2 + core) * 8 + x * 2 + y % 2
            pairs.append((lat * 8 + lon, to))
    return lax.ppermute(array, ("lat", "lon"), pairs)


def other_core(array):
    return lax.ppermute(array, "lat", [(i, i ^ 1) for i in range(16)])


def added(*terms):
    total = terms[0].astype(F32)
    for term in terms[1:]:
        total = total + term.astype(F32)
    return total.astype(BF16)


def scatter_sum(sums):
    held = added(sums[:16], other_core(sums[16:]))
    held = added(held[:4], *[along(held[4 * k : 4 * k + 4], 0, k) for k in (1, 2, 3)])
    return added(held[0], *[along(held[k], 1, k) for k in (1, 2, 3)])


def all_sum(sums_one, sums_two):
    share = jnp.concatenate([scatter_sum(sums_one), scatter_sum(sums_two)], 0)
    share = lax.optimization_barrier(share)
    one, two, three = [along(share, 2, k).astype(F32) for k in (1, 2, 3)]
    share = ((share.astype(F32) + two) + (one + three)).astype(BF16)
    held = jnp.stack([share] + [along(share, 1, k) for k in (1, 2, 3)])
    held = jnp.concatenate([held] + [along(held, 0, k) for k in (1, 2, 3)])
    return jnp.concatenate([held, other_core(held)])


def local(tokens, cotangent, w_qkv, w_proj, w_up, w_down, pair_bias, gain_one, gain_two):
    total_tokens = ROWS * lax.axis_size("lat") * lax.axis_size("lon")
    scale = total_tokens ** (-0.5)
    place = place_of()
    token = jnp.arange(WT, dtype=jnp.int32)
    lower = (token // WLON) % WLAT >= WLAT // 2
    apart = (lower[:, None] != lower[None, :]) & (
        lax.axis_index("lat") == lax.axis_size("lat") - 1
    )
    mask_t = jnp.where(apart, MASKED, 0.0).astype(F32)
    bias_t = jnp.swapaxes(pair_bias, 1, 2)
    gain_one = gain_one.reshape(1, D)
    gain_two = gain_two.reshape(1, D)
    xw, qkv, probs, grad_mixed, grad_res, sums_one, sum_proj, sum_gain_two = forward(
        place, tokens, *halos(tokens), cotangent, *halos(cotangent),
        w_qkv, w_proj, w_up, w_down, bias_t, mask_t, gain_one, gain_two,
    )
    grad_grid, sums_two = backward(
        place, xw, qkv, probs, grad_mixed, grad_res, sum_proj, sum_gain_two, w_qkv, gain_one
    )
    grad_tokens = bring_home(grad_grid)
    sums = all_sum(sums_one, sums_two)
    sum_up, sum_down = finish_one(place, sums, scale)
    sum_qkv, sum_proj, sum_bias, sum_one, sum_two = finish_two(place, sums, scale)
    return (
        grad_tokens,
        sum_qkv,
        sum_proj,
        sum_up,
        sum_down,
        jnp.swapaxes(sum_bias, 1, 2),
        sum_one.reshape(D),
        sum_two.reshape(D),
    )


def solution(mesh):
    grid = P(None, "lat", "lon", None)
    in_specs = (grid, grid, P(), P(), P(), P(), P(), P(), P())
    out_specs = (grid, P(), P(), P(), P(), P(), P(), P())
    return jax.shard_map(local, mesh=mesh, in_specs=in_specs, out_specs=out_specs, check_vma=False)
```

time: 460 us -> 249 us (0.54); the launches traced: 453 us -> 249 us
  Pallas kernels: 0 us -> 114 us
  local copies, waits for them, and re-layouts: 120 us -> 18.8 us
  matrix products: 70.5 us -> 0 us
  blocking collectives: 67.9 us -> 0 us
  waiting for transfers between devices: 118 us -> 60.6 us
  other arithmetic: 51.8 us -> 4.68 us
  starting transfers between devices: 10 us -> 49.9 us
  between operations: 14.9 us -> 0.98 us
    pallas_call x0 -> x4, Pallas kernels: none -> 114 us  [the longest x1 62.6 us: forward(): pl.pallas_call(forward_kernel, out_shape=(shape(ROWS, D), shape(ROWS, QKV...]
    psum x1 -> x0, waiting for transfers between devices: 85.9 us -> none  [local(): lax.psum((mlp_sums[0], mlp_sums[1], mlp_sums[2], mlp_sums[3], attn_sums[0...]
    dot_general x17 -> x0, matrix products: 70.5 us -> none  [the longest x1 8.24 us: mlp_part(): grad_act = jnp.dot(cotan_rows, w_down.T, preferred_element_type=jnp.float32)]
    psum x1 -> x0, blocking collectives: 67.9 us -> none  [local(): lax.psum((mlp_sums[0], mlp_sums[1], mlp_sums[2], mlp_sums[3], attn_sums[0...]
    another operation x6 -> x0, local copies, waits for them, and re-layouts: 42.7 us -> none  [the longest x1 12 us: window_backward(): jnp.stack([grad_query, grad_key, grad_val], 2)]
    ppermute x8 -> x33, starting transfers between devices: 9.97 us -> 49.9 us  [the longest x21 30.2 us: along(): return lax.ppermute(array, ('lat', 'lon'), pairs)]
    ppermute x8 -> x33, waiting for transfers between devices: 32.1 us -> 60.6 us  [the longest x21 49.1 us: along(): return lax.ppermute(array, ('lat', 'lon'), pairs)]
    convert_element_type x3 -> x0, local copies, waits for them, and re-layouts: 20.2 us -> none  [the longest x1 10.7 us: window_backward(): grad_qkv = jnp.stack([grad_query, grad_key, grad_val], 2).reshape(count_w...]
  transfers between devices with their start and end apart: 9 -> 33, of which waited for: 7 -> 16; matrix products, arithmetic and copies ran while one was open for 6% -> 6% of each run, Pallas kernels for 0% -> 14%
where the time goes in v1:
time: 249 us
  Pallas kernels  114 us (46%)
  waiting for transfers between devices  60.6 us (24%)
  starting transfers between devices  49.9 us (20%)
  local copies, waits for them, and re-layouts  18.8 us (8%)
  other arithmetic  4.68 us (2%)
    pallas_call x1, Pallas kernels, forward(): pl.pallas_call(forward_kernel, out_shape=(shape(ROWS, D), shape(ROWS, QKV...  62.6 us
    ppermute x21, waiting for transfers between devices, along(): return lax.ppermute(array, ('lat', 'lon'), pairs)  49.1 us
    pallas_call x1, Pallas kernels, backward(): pl.pallas_call(backward_kernel, out_shape=(shape(LEVELS, HEIGHT, BREADTH,...  33.7 us
    ppermute x21, starting transfers between devices, along(): return lax.ppermute(array, ('lat', 'lon'), pairs)  30.2 us
    ppermute x9, starting transfers between devices, neighbour(): return lax.ppermute(array, ('lat', 'lon'), pairs)  18.8 us
    pallas_call x1, Pallas kernels, finish_one(): pl.pallas_call(functools.partial(finish_one_kernel, scale), out_shape=(sh...  12 us
    unnamed x30, local copies, waits for them, and re-layouts  8.95 us
    ppermute x9, waiting for transfers between devices, neighbour(): return lax.ppermute(array, ('lat', 'lon'), pairs)  8.93 us
  transfers between devices with their start and end apart: 33, of which 16 were waited for; matrix products, arithmetic and copies ran while one was open for 6% of the time, Pallas kernels for 14%

profile of v1, /device:TPU:0, one launch (start us, length us, event | category | flops | bytes accessed | tf_op | source)
XLA Modules:
  0.0 248.7 jit_solution(2911537114071088420)
XLA Ops:
  0.6 0.9 slice.90
  1.6 3.9 %collective-permute-start = (bf16[2,12,6,512]{3,2,1,0:T(8,128)(2,1)S(1)}, bf16[2,12,6,512]{3,2,1,0:T(8,128)(2,1)S(1)}, u32[]{:S(2)}, u32[]{:S(2)}) collective-permute-start(bf16[2,12,6,512]{3,2,1,0:T(8,128)(2,1)S(1)} %slice.90), channel_id=1, source_target_pairs={{0,7},{1,0},{2,1},{3,2},{4,3},{5,4},{6,5},{7,6},{8,15},{9,8},{10,9... | collective-permute-start | bytes 442376 | tf_op jit(solution)/shard_map/ppermute | solution.py:448
  5.5 1.0 slice.91
  6.5 5.6 %collective-permute-start.1 = (bf16[2,3,48,512]{3,2,1,0:T(8,128)(2,1)S(1)}, bf16[2,3,48,512]{3,2,1,0:T(8,128)(2,1)S(1)}, u32[]{:S(2)}, u32[]{:S(2)}) collective-permute-start(bf16[2,3,48,512]{3,2,1,0:T(8,128)(2,1)S(1)} %slice.91), channel_id=1, source_target_pairs={{0,120},{1,121},{2,122},{3,123},{4,124},{5,125},{6,126},{7,127},{8... | collective-permute-start | bytes 884744 | tf_op jit(solution)/shard_map/ppermute | solution.py:448
  12.1 0.8 slice.92
  13.1 0.9 slice.93
  14.1 1.0 collective-permute-start.3
  15.1 1.0 slice.94
  16.1 1.5 collective-permute-start.4
  17.6 0.7 and_select_fusion.mask_t
  18.3 0.8 slice.95
  19.1 3.1 %collective-permute-start.5 = (bf16[2,3,6,512]{3,2,1,0:T(8,128)(2,1)S(1)}, bf16[2,3,6,512]{3,2,1,0:T(8,128)(2,1)S(1)}, u32[]{:S(2)}, u32[]{:S(2)}) collective-permute-start(bf16[2,3,6,512]{3,2,1,0:T(8,128)(2,1)S(1)} %slice.95), channel_id=1, source_target_pairs={{0,127},{1,120},{2,121},{3,122},{4,123},{5,124},{6,125},{7,126},{8... | collective-permute-start | bytes 110600 | tf_op jit(solution)/shard_map/ppermute | solution.py:448
  22.2 0.6 pad_add_fusion.place_ref
  22.8 2.9 %copy.17 = f32[8,144,144]{1,2,0:T(8,128)} copy(f32[8,144,144]{2,1,0:T(8,128)} %param.15) | data formatting | bytes 1327104 | tf_op args[6]
  25.8 0.5 copy-done.10
  26.7 62.6 %forward_mlp.1 = (bf16[1152,512]{1,0:T(8,128)(2,1)}, bf16[1152,1536]{1,0:T(8,128)(2,1)}, bf16[8,8,144,144]{3,2,1,0:T(8,128)(2,1)}, bf16[1152,512]{1,0:T(8,128)(2...) custom-call(s32[4]{0:T(128)} %pad_add_fusion.place_ref, ...), custom_call_target="tpu_custom_call" | custom-call | tf_op jit(solution)/shard_map/forward_mlp/pallas_call | solution.py:358
  89.3 1.8 slice.101
  91.1 33.7 %attention_back.1 = (bf16[2,12,48,512]{3,2,1,0:T(8,128)(2,1)}, bf16[32,304,128]{2,1,0:T(8,128)(2,1)}) custom-call(s32[4]{0:T(128)} %pad_add_fusion.place_ref, bf16[1152,512]{1,0:T(8,128)(2,1)} %get-tuple-element.25.xw, bf16[1152,1536]{1,0:T(8,128)(2,1)} %get-tuple-element.26.qkv, bf16[8,8,144,144]{3,2,1,0:T(8,128)(2,1)} %get-tuple-element.27.probs, ...), custom_call_target="tpu_custom_call" | custom-call | tf_op jit(solution)/shard_map/attention_back/pallas_call | solution.py:385
  124.8 1.5 slice.111
  126.4 0.8 collective-permute-start.16
  127.1 2.6 %collective-permute-done.16 = bf16[16,304,128]{2,1,0:T(8,128)(2,1)S(1)} collective-permute-done((bf16[16,304,128]{2,1,0:T(8,128)(2,1)S(1)}, bf16[16,304,128]{2,1,0:T(8,128)(2,1)S(1)}, u32[]{:S(2)}, u32[]{:S(2)}) %collective-permute-start.16) | collective-permute-done | bytes 1245216 | tf_op jit(solution)/shard_map/ppermute | solution.py:497
  129.7 0.3 add_convert_fusion.1
  130.1 1.3 collective-permute-start.19
  131.4 1.9 collective-permute-start.18
  133.3 0.6 add_convert_fusion
  133.9 3.3 %collective-permute-start.12 = (bf16[4,512,128]{2,1,0:T(8,128)(2,1)S(1)}, bf16[4,512,128]{2,1,0:T(8,128)(2,1)S(1)}, u32[]{:S(2)}, u32[]{:S(2)}) collective-permute-start(bf16[4,512,128]{2,1,0:T(8,128)(2,1)S(1)} %get-tuple-element.53), channel_id=1, source_target_pairs={{0,6},{1,7},{2,0},{3,1},{4,2},{5,3},{6,4},{7,5},{8,25},{9,8},{10,2... | collective-permute-start | bytes 1572872 | tf_op jit(solution)/shard_map/ppermute | solution.py:493
  137.2 0.4 collective-permute-start.11
  137.7 3.8 %collective-permute-start.10 = (bf16[4,512,128]{2,1,0:T(8,128)(2,1)S(1)}, bf16[4,512,128]{2,1,0:T(8,128)(2,1)S(1)}, u32[]{:S(2)}, u32[]{:S(2)}) collective-permute-start(bf16[4,512,128]{2,1,0:T(8,128)(2,1)S(1)} %get-tuple-element.52), channel_id=1, source_target_pairs={{0,2},{1,3},{2,4},{3,5},{4,6},{5,7},{6,0},{7,1},{8,9},{9,24},{10,1... | collective-permute-start | bytes 1572872 | tf_op jit(solution)/shard_map/ppermute | solution.py:493
  141.4 1.7 collective-permute-done.17
  143.3 1.0 collective-permute-start.22
  144.3 1.1 collective-permute-start.21
  145.3 0.7 collective-permute-done.12
  146.0 1.1 collective-permute-start.20
  147.1 1.8 collective-permute-done.11
  148.9 5.5 %collective-permute-done.10 = bf16[4,512,128]{2,1,0:T(8,128)(2,1)S(1)} collective-permute-done((bf16[4,512,128]{2,1,0:T(8,128)(2,1)S(1)}, bf16[4,512,128]{2,1,0:T(8,128)(2,1)S(1)}, u32[]{:S(2)}, u32[]{:S(2)}) %collective-permute-start.10) | collective-permute-done | bytes 524320 | tf_op jit(solution)/shard_map/ppermute | solution.py:493
  154.7 1.0 collective-permute-start.15
  155.7 1.0 collective-permute-start.14
  156.7 1.3 collective-permute-start.13
  158.1 1.6 collective-permute-done.15
  159.7 2.5 %collective-permute-done.14 = bf16[512,128]{1,0:T(8,128)(2,1)S(1)} collective-permute-done((bf16[512,128]{1,0:T(8,128)(2,1)S(1)}, bf16[512,128]{1,0:T(8,128)(2,1)S(1)}, u32[]{:S(2)}, u32[]{:S(2)}) %collective-permute-start.14) | collective-permute-done | bytes 131104 | tf_op jit(solution)/shard_map/ppermute | solution.py:493
  162.2 1.3 collective-permute-done.13
  163.7 4.8 %collective-permute-start.25 = (bf16[816,128]{1,0:T(8,128)(2,1)S(1)}, bf16[816,128]{1,0:T(8,128)(2,1)S(1)}, u32[]{:S(2)}, u32[]{:S(2)}) collective-permute-start(bf16[816,128]{1,0:T(8,128)(2,1)S(1)} %pad_maximum_fusion.1), channel_id=1, source_target_pairs={{0,96},{1,97},{2,98},{3,99},{4,100},{5,101},{6,102},{7,103},{8,14}... | collective-permute-start | bytes 626696 | tf_op jit(solution)/shard_map/ppermute | solution.py:493
  168.4 1.5 collective-permute-start.23
  170.0 1.8 collective-permute-done.25
  171.7 5.9 %collective-permute-done.24 = bf16[816,128]{1,0:T(8,128)(2,1)S(1)} collective-permute-done((bf16[816,128]{1,0:T(8,128)(2,1)S(1)}, bf16[816,128]{1,0:T(8,128)(2,1)S(1)}, u32[]{:S(2)}, u32[]{:S(2)}) %collective-permute-start.24) | collective-permute-done | bytes 208928 | tf_op jit(solution)/shard_map/ppermute | solution.py:493
  177.9 2.1 collective-permute-start.27
  180.0 1.2 collective-permute-start.28
  181.2 5.9 %collective-permute-done.26 = bf16[816,128]{1,0:T(8,128)(2,1)S(1)} collective-permute-done((bf16[816,128]{1,0:T(8,128)(2,1)S(1)}, bf16[816,128]{1,0:T(8,128)(2,1)S(1)}, u32[]{:S(2)}, u32[]{:S(2)}) %collective-permute-start.26) | collective-permute-done | bytes 208928 | tf_op jit(solution)/shard_map/ppermute | solution.py:493
  187.1 0.9 collective-permute-done.28
  188.2 2.5 %collective-permute-start.30 = (bf16[4,816,128]{2,1,0:T(8,128)(2,1)S(1)}, bf16[4,816,128]{2,1,0:T(8,128)(2,1)S(1)}, u32[]{:S(2)}, u32[]{:S(2)}) collective-permute-start(bf16[4,816,128]{2,1,0:T(8,128)(2,1)S(1)} %pad_maximum_fusion), channel_id=1, source_target_pairs={{0,4},{1,5},{2,6},{3,7},{4,0},{5,1},{6,2},{7,3},{8,24},{9,25},{10,... | collective-permute-start | bytes 2506760 | tf_op jit(solution)/shard_map/ppermute | solution.py:493
  190.7 0.9 collective-permute-start.31
  191.8 19.1 %collective-permute-done.29 = bf16[4,816,128]{2,1,0:T(8,128)(2,1)S(1)} collective-permute-done((bf16[4,816,128]{2,1,0:T(8,128)(2,1)S(1)}, bf16[4,816,128]{2,1,0:T(8,128)(2,1)S(1)}, u32[]{:S(2)}, u32[]{:S(2)}) %collective-permute-start.29) | collective-permute-done | bytes 835616 | tf_op jit(solution)/shard_map/ppermute | solution.py:493
  210.9 0.3 constant_dynamic-update-slice_fusion.2
  211.2 0.3 constant_dynamic-update-slice_fusion.1
  211.5 0.3 collective-permute-done.31
  212.3 0.6 collective-permute-start.7
  213.0 2.8 %collective-permute-start.6 = (bf16[2,3,6,512]{3,2,1,0:T(8,128)(2,1)S(1)}, bf16[2,3,6,512]{3,2,1,0:T(8,128)(2,1)S(1)}, u32[]{:S(2)}, u32[]{:S(2)}) collective-permute-start(bf16[2,3,6,512]{3,2,1,0:T(8,128)(2,1)S(1)} %slice.96), channel_id=1, source_target_pairs={{0,9},{1,10},{2,11},{3,12},{4,13},{5,14},{6,15},{7,8},{8,17},{9,18... | collective-permute-start | bytes 110600 | tf_op jit(solution)/shard_map/ppermute | solution.py:448
  215.9 8.8 %collective-permute-done.6 = bf16[2,3,6,512]{3,2,1,0:T(8,128)(2,1)S(1)} collective-permute-done((bf16[2,3,6,512]{3,2,1,0:T(8,128)(2,1)S(1)}, bf16[2,3,6,512]{3,2,1,0:T(8,128)(2,1)S(1)}, u32[]{:S(2)}, u32[]{:S(2)}) %collective-permute-start.6) | collective-permute-done | bytes 36896 | tf_op jit(solution)/shard_map/ppermute | solution.py:448
  224.8 1.6 maximum_maximum_fusion
  226.4 0.4 constant_dynamic-update-slice_fusion.7.sums.up_in.down_in
  226.9 2.7 %copy-done = bf16[32,816,128]{2,1,0:T(8,128)(2,1)} copy-done((bf16[32,816,128]{2,1,0:T(8,128)(2,1)}, bf16[32,816,128]{2,1,0:T(8,128)(2,1)S(1)}, u32[]{:S(2)}) %copy-start) | copy-done | bytes 6684696
  229.6 5.5 %finish_attention.1 = (f32[512,1536]{1,0:T(8,128)}, f32[512,512]{1,0:T(8,128)}, f32[8,144,144]{2,1,0:T(8,128)}, f32[1,512]{1,0:T(1,128)}, f32[1,512]{1,0:T(1,128)}) custom-call(s32[4]{0:T(128)} %pad_add_fusion.place_ref, bf16[32,816,128]{2,1,0:T(8,128)(2,1)} %copy-done), custom_call_target="tpu_custom_call" | custom-call | tf_op jit(solution)/shard_map/finish_attention/pallas_call | solution.py:425
  235.1 12.0 %finish_mlp.1 = (f32[512,2048]{1,0:T(8,128)}, f32[2048,512]{1,0:T(8,128)}) custom-call(s32[4]{0:T(128)} %pad_add_fusion.place_ref, bf16[32,816,128]{2,1,0:T(8,128)(2,1)} %copy-done, bf16[32,816,128]{2,1,0:T(8,128)(2,1)} %copy-done), custom_call_target="tpu_custom_call" | custom-call | tf_op jit(solution)/shard_map/finish_mlp/pallas_call | solution.py:404
  247.1 1.6 copy.18
  (67 shorter events, 2.9 us)
Async XLA Ops:
  1.6 24.1 %collective-permute-start = (bf16[2,12,6,512]{3,2,1,0:T(8,128)(2,1)S(1)}, bf16[2,12,6,512]{3,2,1,0:T(8,128)(2,1)S(1)}, u32[]{:S(2)}, u32[]{:S(2)}) collective-permute-start(bf16[2,12,6,512]{3,2,1,0:T(8,128)(2,1)S(1)} %slice.90), channel_id=1, source_target_pairs={{0,7},{1,0},{2,1},{3,2},{4,3},{5,4},{6,5},{7,6},{8,15},{9,8},{10,9... | collective-permute-start | bytes 442376 | tf_op jit(solution)/shard_map/ppermute | solution.py:448
  6.5 19.3 %collective-permute-start.1 = (bf16[2,3,48,512]{3,2,1,0:T(8,128)(2,1)S(1)}, bf16[2,3,48,512]{3,2,1,0:T(8,128)(2,1)S(1)}, u32[]{:S(2)}, u32[]{:S(2)}) collective-permute-start(bf16[2,3,48,512]{3,2,1,0:T(8,128)(2,1)S(1)} %slice.91), channel_id=1, source_target_pairs={{0,120},{1,121},{2,122},{3,123},{4,124},{5,125},{6,126},{7,127},{8... | collective-permute-start | bytes 884744 | tf_op jit(solution)/shard_map/ppermute | solution.py:448
  12.9 6.2 %collective-permute-start.2 = (bf16[2,3,6,512]{3,2,1,0:T(8,128)(2,1)S(1)}, bf16[2,3,6,512]{3,2,1,0:T(8,128)(2,1)S(1)}, u32[]{:S(2)}, u32[]{:S(2)}) collective-permute-start(bf16[2,3,6,512]{3,2,1,0:T(8,128)(2,1)S(1)} %slice.92), channel_id=1, source_target_pairs={{0,127},{1,120},{2,121},{3,122},{4,123},{5,124},{6,125},{7,126},{8... | collective-permute-start | bytes 110600 | tf_op jit(solution)/shard_map/ppermute | solution.py:448
  14.1 11.7 %collective-permute-start.3 = (bf16[2,12,6,512]{3,2,1,0:T(8,128)(2,1)S(1)}, bf16[2,12,6,512]{3,2,1,0:T(8,128)(2,1)S(1)}, u32[]{:S(2)}, u32[]{:S(2)}) collective-permute-start(bf16[2,12,6,512]{3,2,1,0:T(8,128)(2,1)S(1)} %slice.93), channel_id=1, source_target_pairs={{0,7},{1,0},{2,1},{3,2},{4,3},{5,4},{6,5},{7,6},{8,15},{9,8},{10,9... | collective-permute-start | bytes 442376 | tf_op jit(solution)/shard_map/ppermute | solution.py:448
  16.1 9.7 %collective-permute-start.4 = (bf16[2,3,48,512]{3,2,1,0:T(8,128)(2,1)S(1)}, bf16[2,3,48,512]{3,2,1,0:T(8,128)(2,1)S(1)}, u32[]{:S(2)}, u32[]{:S(2)}) collective-permute-start(bf16[2,3,48,512]{3,2,1,0:T(8,128)(2,1)S(1)} %slice.94), channel_id=1, source_target_pairs={{0,120},{1,121},{2,122},{3,123},{4,124},{5,125},{6,126},{7,127},{8... | collective-permute-start | bytes 884744 | tf_op jit(solution)/shard_map/ppermute | solution.py:448
  19.1 6.7 %copy-start.9 = (bf16[2,3,6,512]{3,2,1,0:T(8,128)(2,1)}, bf16[2,3,6,512]{3,2,1,0:T(8,128)(2,1)S(1)}, u32[]{:S(2)}) copy-start(bf16[2,3,6,512]{3,2,1,0:T(8,128)(2,1)S(1)} %collective-permute-done.2.tok_both) | copy-start | bytes 110596
  19.1 6.6 %collective-permute-start.5 = (bf16[2,3,6,512]{3,2,1,0:T(8,128)(2,1)S(1)}, bf16[2,3,6,512]{3,2,1,0:T(8,128)(2,1)S(1)}, u32[]{:S(2)}, u32[]{:S(2)}) collective-permute-start(bf16[2,3,6,512]{3,2,1,0:T(8,128)(2,1)S(1)} %slice.95), channel_id=1, source_target_pairs={{0,127},{1,120},{2,121},{3,122},{4,123},{5,124},{6,125},{7,126},{8... | collective-permute-start | bytes 110600 | tf_op jit(solution)/shard_map/ppermute | solution.py:448
  25.7 0.6 copy-start.10
  25.7 0.7 copy-start.7
  25.7 0.7 copy-start.8
  25.8 0.8 copy-start.5
  25.8 0.9 copy-start.6
  91.0 42.2 %collective-permute-start.9 = (bf16[16,512,128]{2,1,0:T(8,128)(2,1)S(1)}, bf16[16,512,128]{2,1,0:T(8,128)(2,1)S(1)}, u32[]{:S(2)}, u32[]{:S(2)}) collective-permute-start(bf16[16,512,128]{2,1,0:T(8,128)(2,1)S(1)} %slice.101), channel_id=1, source_target_pairs={{0,8},{8,0},{16,24},{24,16},{32,40},{40,32},{48,56},{56,48},{64,72... | collective-permute-start | bytes 6291464 | tf_op jit(solution)/shard_map/ppermute | solution.py:497
  124.8 4.9 %copy-start.2 = (bf16[32,304,128]{2,1,0:T(8,128)(2,1)S(1)}, bf16[32,304,128]{2,1,0:T(8,128)(2,1)}, u32[]{:S(2)}) copy-start(bf16[32,304,128]{2,1,0:T(8,128)(2,1)} %get-tuple-element.34) | copy-start | bytes 7471108
  126.4 6.9 %copy-start.1 = (bf16[32,512,128]{2,1,0:T(8,128)(2,1)S(1)}, bf16[32,512,128]{2,1,0:T(8,128)(2,1)}, u32[]{:S(2)}) copy-start(bf16[32,512,128]{2,1,0:T(8,128)(2,1)} %get-tuple-element.33) | copy-start | bytes 12582916
  126.4 3.3 %collective-permute-start.16 = (bf16[16,304,128]{2,1,0:T(8,128)(2,1)S(1)}, bf16[16,304,128]{2,1,0:T(8,128)(2,1)S(1)}, u32[]{:S(2)}, u32[]{:S(2)}) collective-permute-start(bf16[16,304,128]{2,1,0:T(8,128)(2,1)S(1)} %slice.111), channel_id=1, source_target_pairs={{0,8},{8,0},{16,24},{24,16},{32,40},{40,32},{48,56},{56,48},{64,72... | collective-permute-start | bytes 3735560 | tf_op jit(solution)/shard_map/ppermute | solution.py:497
  130.1 7.6 %collective-permute-start.19 = (bf16[4,304,128]{2,1,0:T(8,128)(2,1)S(1)}, bf16[4,304,128]{2,1,0:T(8,128)(2,1)S(1)}, u32[]{:S(2)}, u32[]{:S(2)}) collective-permute-start(bf16[4,304,128]{2,1,0:T(8,128)(2,1)S(1)} %get-tuple-element.56), channel_id=1, source_target_pairs={{0,6},{1,7},{2,0},{3,1},{4,2},{5,3},{6,4},{7,5},{8,25},{9,8},{10,2... | collective-permute-start | bytes 933896 | tf_op jit(solution)/shard_map/ppermute | solution.py:493
  131.4 10.1 %collective-permute-start.18 = (bf16[4,304,128]{2,1,0:T(8,128)(2,1)S(1)}, bf16[4,304,128]{2,1,0:T(8,128)(2,1)S(1)}, u32[]{:S(2)}, u32[]{:S(2)}) collective-permute-start(bf16[4,304,128]{2,1,0:T(8,128)(2,1)S(1)} %get-tuple-element.57), channel_id=1, source_target_pairs={{0,4},{1,5},{2,6},{3,7},{4,0},{5,1},{6,2},{7,3},{8,24},{9,25},{10,... | collective-permute-start | bytes 933896 | tf_op jit(solution)/shard_map/ppermute | solution.py:493
  133.3 9.8 %collective-permute-start.17 = (bf16[4,304,128]{2,1,0:T(8,128)(2,1)S(1)}, bf16[4,304,128]{2,1,0:T(8,128)(2,1)S(1)}, u32[]{:S(2)}, u32[]{:S(2)}) collective-permute-start(bf16[4,304,128]{2,1,0:T(8,128)(2,1)S(1)} %get-tuple-element.55), channel_id=1, source_target_pairs={{0,2},{1,3},{2,4},{3,5},{4,6},{5,7},{6,0},{7,1},{8,9},{9,24},{10,1... | collective-permute-start | bytes 933896 | tf_op jit(solution)/shard_map/ppermute | solution.py:493
  133.9 12.1 %collective-permute-start.12 = (bf16[4,512,128]{2,1,0:T(8,128)(2,1)S(1)}, bf16[4,512,128]{2,1,0:T(8,128)(2,1)S(1)}, u32[]{:S(2)}, u32[]{:S(2)}) collective-permute-start(bf16[4,512,128]{2,1,0:T(8,128)(2,1)S(1)} %get-tuple-element.53), channel_id=1, source_target_pairs={{0,6},{1,7},{2,0},{3,1},{4,2},{5,3},{6,4},{7,5},{8,25},{9,8},{10,2... | collective-permute-start | bytes 1572872 | tf_op jit(solution)/shard_map/ppermute | solution.py:493
  137.2 11.6 %collective-permute-start.11 = (bf16[4,512,128]{2,1,0:T(8,128)(2,1)S(1)}, bf16[4,512,128]{2,1,0:T(8,128)(2,1)S(1)}, u32[]{:S(2)}, u32[]{:S(2)}) collective-permute-start(bf16[4,512,128]{2,1,0:T(8,128)(2,1)S(1)} %get-tuple-element.54), channel_id=1, source_target_pairs={{0,4},{1,5},{2,6},{3,7},{4,0},{5,1},{6,2},{7,3},{8,24},{9,25},{10,... | collective-permute-start | bytes 1572872 | tf_op jit(solution)/shard_map/ppermute | solution.py:493
  137.7 16.7 %collective-permute-start.10 = (bf16[4,512,128]{2,1,0:T(8,128)(2,1)S(1)}, bf16[4,512,128]{2,1,0:T(8,128)(2,1)S(1)}, u32[]{:S(2)}, u32[]{:S(2)}) collective-permute-start(bf16[4,512,128]{2,1,0:T(8,128)(2,1)S(1)} %get-tuple-element.52), channel_id=1, source_target_pairs={{0,2},{1,3},{2,4},{3,5},{4,6},{5,7},{6,0},{7,1},{8,9},{9,24},{10,1... | collective-permute-start | bytes 1572872 | tf_op jit(solution)/shard_map/ppermute | solution.py:493
  143.3 13.4 %collective-permute-start.22 = (bf16[304,128]{1,0:T(8,128)(2,1)S(1)}, bf16[304,128]{1,0:T(8,128)(2,1)S(1)}, u32[]{:S(2)}, u32[]{:S(2)}) collective-permute-start(bf16[304,128]{1,0:T(8,128)(2,1)S(1)} %get-tuple-element.68), channel_id=1, source_target_pairs={{0,17},{1,0},{2,19},{3,2},{4,21},{5,4},{6,23},{7,6},{8,104},{9,105... | collective-permute-start | bytes 233480 | tf_op jit(solution)/shard_map/ppermute | solution.py:493
  144.3 13.7 %collective-permute-start.21 = (bf16[304,128]{1,0:T(8,128)(2,1)S(1)}, bf16[304,128]{1,0:T(8,128)(2,1)S(1)}, u32[]{:S(2)}, u32[]{:S(2)}) collective-permute-start(bf16[304,128]{1,0:T(8,128)(2,1)S(1)} %get-tuple-element.69), channel_id=1, source_target_pairs={{0,16},{1,17},{2,18},{3,19},{4,20},{5,21},{6,22},{7,23},{8,72},{9,... | collective-permute-start | bytes 233480 | tf_op jit(solution)/shard_map/ppermute | solution.py:493
  146.0 12.0 %collective-permute-start.20 = (bf16[304,128]{1,0:T(8,128)(2,1)S(1)}, bf16[304,128]{1,0:T(8,128)(2,1)S(1)}, u32[]{:S(2)}, u32[]{:S(2)}) collective-permute-start(bf16[304,128]{1,0:T(8,128)(2,1)S(1)} %get-tuple-element.67), channel_id=1, source_target_pairs={{0,1},{1,16},{2,3},{3,18},{4,5},{5,20},{6,7},{7,22},{8,40},{9,41},... | collective-permute-start | bytes 233480 | tf_op jit(solution)/shard_map/ppermute | solution.py:493
  154.7 5.0 %collective-permute-start.15 = (bf16[512,128]{1,0:T(8,128)(2,1)S(1)}, bf16[512,128]{1,0:T(8,128)(2,1)S(1)}, u32[]{:S(2)}, u32[]{:S(2)}) collective-permute-start(bf16[512,128]{1,0:T(8,128)(2,1)S(1)} %get-tuple-element.65), channel_id=1, source_target_pairs={{0,17},{1,0},{2,19},{3,2},{4,21},{5,4},{6,23},{7,6},{8,104},{9,105... | collective-permute-start | bytes 393224 | tf_op jit(solution)/shard_map/ppermute | solution.py:493
  155.7 6.5 %collective-permute-start.14 = (bf16[512,128]{1,0:T(8,128)(2,1)S(1)}, bf16[512,128]{1,0:T(8,128)(2,1)S(1)}, u32[]{:S(2)}, u32[]{:S(2)}) collective-permute-start(bf16[512,128]{1,0:T(8,128)(2,1)S(1)} %get-tuple-element.66), channel_id=1, source_target_pairs={{0,16},{1,17},{2,18},{3,19},{4,20},{5,21},{6,22},{7,23},{8,72},{9,... | collective-permute-start | bytes 393224 | tf_op jit(solution)/shard_map/ppermute | solution.py:493
  156.7 6.9 %collective-permute-start.13 = (bf16[512,128]{1,0:T(8,128)(2,1)S(1)}, bf16[512,128]{1,0:T(8,128)(2,1)S(1)}, u32[]{:S(2)}, u32[]{:S(2)}) collective-permute-start(bf16[512,128]{1,0:T(8,128)(2,1)S(1)} %get-tuple-element.64), channel_id=1, source_target_pairs={{0,1},{1,16},{2,3},{3,18},{4,5},{5,20},{6,7},{7,22},{8,40},{9,41},... | collective-permute-start | bytes 393224 | tf_op jit(solution)/shard_map/ppermute | solution.py:493
  163.7 8.1 %collective-permute-start.25 = (bf16[816,128]{1,0:T(8,128)(2,1)S(1)}, bf16[816,128]{1,0:T(8,128)(2,1)S(1)}, u32[]{:S(2)}, u32[]{:S(2)}) collective-permute-start(bf16[816,128]{1,0:T(8,128)(2,1)S(1)} %pad_maximum_fusion.1), channel_id=1, source_target_pairs={{0,96},{1,97},{2,98},{3,99},{4,100},{5,101},{6,102},{7,103},{8,14}... | collective-permute-start | bytes 626696 | tf_op jit(solution)/shard_map/ppermute | solution.py:493
  168.4 9.3 %collective-permute-start.24 = (bf16[816,128]{1,0:T(8,128)(2,1)S(1)}, bf16[816,128]{1,0:T(8,128)(2,1)S(1)}, u32[]{:S(2)}, u32[]{:S(2)}) collective-permute-start(bf16[816,128]{1,0:T(8,128)(2,1)S(1)} %pad_maximum_fusion.1), channel_id=1, source_target_pairs={{0,32},{1,33},{2,34},{3,35},{4,36},{5,37},{6,38},{7,39},{8,10},{9,... | collective-permute-start | bytes 626696 | tf_op jit(solution)/shard_map/ppermute | solution.py:493
  168.4 9.3 %collective-permute-start.23 = (bf16[816,128]{1,0:T(8,128)(2,1)S(1)}, bf16[816,128]{1,0:T(8,128)(2,1)S(1)}, u32[]{:S(2)}, u32[]{:S(2)}) collective-permute-start(bf16[816,128]{1,0:T(8,128)(2,1)S(1)} %pad_maximum_fusion.1), channel_id=1, source_target_pairs={{0,64},{1,65},{2,66},{3,67},{4,68},{5,69},{6,70},{7,71},{8,12},{9,... | collective-permute-start | bytes 626696 | tf_op jit(solution)/shard_map/ppermute | solution.py:493
  177.8 9.3 %collective-permute-start.26 = (bf16[816,128]{1,0:T(8,128)(2,1)S(1)}, bf16[816,128]{1,0:T(8,128)(2,1)S(1)}, u32[]{:S(2)}, u32[]{:S(2)}) collective-permute-start(bf16[816,128]{1,0:T(8,128)(2,1)S(1)} %get-tuple-element.51), channel_id=1, source_target_pairs={{0,1},{1,16},{2,3},{3,18},{4,5},{5,20},{6,7},{7,22},{8,40},{9,41},... | collective-permute-start | bytes 626696 | tf_op jit(solution)/shard_map/ppermute | solution.py:493
  177.9 9.2 %collective-permute-start.27 = (bf16[816,128]{1,0:T(8,128)(2,1)S(1)}, bf16[816,128]{1,0:T(8,128)(2,1)S(1)}, u32[]{:S(2)}, u32[]{:S(2)}) collective-permute-start(bf16[816,128]{1,0:T(8,128)(2,1)S(1)} %get-tuple-element.51), channel_id=1, source_target_pairs={{0,16},{1,17},{2,18},{3,19},{4,20},{5,21},{6,22},{7,23},{8,72},{9,... | collective-permute-start | bytes 626696 | tf_op jit(solution)/shard_map/ppermute | solution.py:493
  180.0 8.0 %collective-permute-start.28 = (bf16[816,128]{1,0:T(8,128)(2,1)S(1)}, bf16[816,128]{1,0:T(8,128)(2,1)S(1)}, u32[]{:S(2)}, u32[]{:S(2)}) collective-permute-start(bf16[816,128]{1,0:T(8,128)(2,1)S(1)} %get-tuple-element.51), channel_id=1, source_target_pairs={{0,17},{1,0},{2,19},{3,2},{4,21},{5,4},{6,23},{7,6},{8,104},{9,105... | collective-permute-start | bytes 626696 | tf_op jit(solution)/shard_map/ppermute | solution.py:493
  188.1 22.7 %collective-permute-start.29 = (bf16[4,816,128]{2,1,0:T(8,128)(2,1)S(1)}, bf16[4,816,128]{2,1,0:T(8,128)(2,1)S(1)}, u32[]{:S(2)}, u32[]{:S(2)}) collective-permute-start(bf16[4,816,128]{2,1,0:T(8,128)(2,1)S(1)} %pad_maximum_fusion), channel_id=1, source_target_pairs={{0,2},{1,3},{2,4},{3,5},{4,6},{5,7},{6,0},{7,1},{8,9},{9,24},{10,1... | collective-permute-start | bytes 2506760 | tf_op jit(solution)/shard_map/ppermute | solution.py:493
  188.2 23.0 %collective-permute-start.30 = (bf16[4,816,128]{2,1,0:T(8,128)(2,1)S(1)}, bf16[4,816,128]{2,1,0:T(8,128)(2,1)S(1)}, u32[]{:S(2)}, u32[]{:S(2)}) collective-permute-start(bf16[4,816,128]{2,1,0:T(8,128)(2,1)S(1)} %pad_maximum_fusion), channel_id=1, source_target_pairs={{0,4},{1,5},{2,6},{3,7},{4,0},{5,1},{6,2},{7,3},{8,24},{9,25},{10,... | collective-permute-start | bytes 2506760 | tf_op jit(solution)/shard_map/ppermute | solution.py:493
  190.7 21.1 %collective-permute-start.31 = (bf16[4,816,128]{2,1,0:T(8,128)(2,1)S(1)}, bf16[4,816,128]{2,1,0:T(8,128)(2,1)S(1)}, u32[]{:S(2)}, u32[]{:S(2)}) collective-permute-start(bf16[4,816,128]{2,1,0:T(8,128)(2,1)S(1)} %pad_maximum_fusion), channel_id=1, source_target_pairs={{0,6},{1,7},{2,0},{3,1},{4,2},{5,3},{6,4},{7,5},{8,25},{9,8},{10,2... | collective-permute-start | bytes 2506760 | tf_op jit(solution)/shard_map/ppermute | solution.py:493
  210.9 1.4 copy-start.3
  212.2 14.2 %collective-permute-start.32 = (bf16[16,816,128]{2,1,0:T(8,128)(2,1)S(1)}, bf16[16,816,128]{2,1,0:T(8,128)(2,1)S(1)}, u32[]{:S(2)}, u32[]{:S(2)}) collective-permute-start(bf16[16,816,128]{2,1,0:T(8,128)(2,1)S(1)} %get-tuple-element.58), channel_id=1, source_target_pairs={{0,8},{8,0},{16,24},{24,16},{32,40},{40,32},{48,56},{56,48},{64,72... | collective-permute-start | bytes 10027016 | tf_op jit(solution)/shard_map/ppermute | solution.py:497
  212.3 12.5 %collective-permute-start.7 = (bf16[2,3,42,512]{3,2,1,0:T(8,128)(2,1)S(1)}, bf16[2,3,42,512]{3,2,1,0:T(8,128)(2,1)S(1)}, u32[]{:S(2)}, u32[]{:S(2)}) collective-permute-start(bf16[2,3,42,512]{3,2,1,0:T(8,128)(2,1)S(1)} %slice.97), channel_id=1, source_target_pairs={{0,8},{1,9},{2,10},{3,11},{4,12},{5,13},{6,14},{7,15},{8,16},{9,17... | collective-permute-start | bytes 774152 | tf_op jit(solution)/shard_map/ppermute | solution.py:448
  212.9 11.7 %collective-permute-start.8 = (bf16[2,9,6,512]{3,2,1,0:T(8,128)(2,1)S(1)}, bf16[2,9,6,512]{3,2,1,0:T(8,128)(2,1)S(1)}, u32[]{:S(2)}, u32[]{:S(2)}) collective-permute-start(bf16[2,9,6,512]{3,2,1,0:T(8,128)(2,1)S(1)} %slice.98), channel_id=1, source_target_pairs={{0,1},{1,2},{2,3},{3,4},{4,5},{5,6},{6,7},{7,0},{8,9},{9,10},{10,1... | collective-permute-start | bytes 331784 | tf_op jit(solution)/shard_map/ppermute | solution.py:448
  213.0 11.6 %collective-permute-start.6 = (bf16[2,3,6,512]{3,2,1,0:T(8,128)(2,1)S(1)}, bf16[2,3,6,512]{3,2,1,0:T(8,128)(2,1)S(1)}, u32[]{:S(2)}, u32[]{:S(2)}) collective-permute-start(bf16[2,3,6,512]{3,2,1,0:T(8,128)(2,1)S(1)} %slice.96), channel_id=1, source_target_pairs={{0,9},{1,10},{2,11},{3,12},{4,13},{5,14},{6,15},{7,8},{8,17},{9,18... | collective-permute-start | bytes 110600 | tf_op jit(solution)/shard_map/ppermute | solution.py:448
  226.9 2.7 %copy-start = (bf16[32,816,128]{2,1,0:T(8,128)(2,1)}, bf16[32,816,128]{2,1,0:T(8,128)(2,1)S(1)}, u32[]{:S(2)}) copy-start(bf16[32,816,128]{2,1,0:T(8,128)(2,1)S(1)} %constant_dynamic-update-slice_fusion.7.sums.up_in.down_in) | copy-start | bytes 20054020
  235.1 12.0 %copy-start.4 = (f32[8,144,144]{2,1,0:T(8,128)S(1)}, f32[8,144,144]{2,1,0:T(8,128)}, u32[]{:S(2)}) copy-start(f32[8,144,144]{2,1,0:T(8,128)} %get-tuple-element.39) | copy-start | bytes 1990660
